TPU v7x, 32 devices: a whole 2x2x4 slice. The times are simulated.
32 devices in a mesh: dp: 4 (over z), expert: 8 (over y, x, core).
Axes of the slice: x: 2, y: 2, z: 4, core: 2. Of those that a mesh axis runs over, the one named last changes fastest.
Arguments:
- tokens: bfloat16 [4096, 2048], P(('dp', 'expert')), may hold values from -6 to 6
- expert_ids: int32 [4096, 6], P(('dp', 'expert')), may hold values from 0 to 15, all different within a row; in each aligned block of 128 rows (0 to 127, 128 to 255, ...) at most 64 rows name the same one
- combine_weight: float32 [4096, 6], P(('dp', 'expert')), may hold values from 0.05 to 1
- partner: int32 [8], replicated, may hold values from 0 to 7, as said below
- w_up: bfloat16 [2048, 16, 768], P(None, 'expert'), may hold values from -0.125 to 0.125
- w_down: bfloat16 [2048, 16, 768], P(None, 'expert'), may hold values from -0.21875 to 0.21875
- out_grad: bfloat16 [4096, 2048], P(('dp', 'expert')), may hold values from -6 to 6
Outputs:
- output: bfloat16 [4096, 2048], P(('dp', 'expert'))
- input_grad: bfloat16 [4096, 2048], P(('dp', 'expert'))
- grad_up: bfloat16 [2048, 16, 768], P('dp', 'expert')
- grad_down: bfloat16 [2048, 16, 768], P('dp', 'expert')
Inputs may be any that keep to these rules, and one draw needn't show every extreme that they name: `expert_ids`: each token names 6 different experts; among the tokens of one device (aligned blocks of 128 tokens) no expert is named more than 64 times, and in some blocks one is named exactly 64 times. partner[partner[j]] = j and partner[j] != j for every j.
All inputs are finite; a program needn't handle non-finite values.
Results may differ from a plain program's by a relative error of at most 0.017.
Values may be sent and summed in bfloat16 or wider, within the bound.
No kernel may reach another device: no remote copies, remote signals or barrier semaphores. Data moves between devices by JAX's collectives and lax.ppermute only.
A program may use at most 192 MiB of HBM per device.

v0:
```python
import functools

import jax
import jax.numpy as jnp
from jax import lax
from jax.experimental import pallas as pl
from jax.experimental.pallas import tpu as pltpu
from jax.sharding import PartitionSpec as P

F32 = jnp.float32
BF16 = jnp.bfloat16
MIB = 1 << 20


def swap(x, axis, mask):
    size = lax.axis_size(axis)
    return lax.ppermute(x, axis, [(i, i ^ mask) for i in range(size)])


def zero_of(x):
    first = lax.slice(x, (0,) * x.ndim, (1,) * x.ndim).reshape(()).astype(F32)
    return jnp.minimum(jnp.abs(first), 0.0)


def after(x, *given):
    total = sum(zero_of(one) for one in given)
    return x + total.astype(x.dtype)


def block_order(groups):
    top = groups // 2
    order = []
    bit = 1
    while bit < top:
        step = [m for m in range(groups) if m & bit and not m & (bit - 1)]
        order += [m for m in step if m & top] + [m for m in step if not m & top]
        bit *= 2
    return order + [top, 0]


def relative_cols(x, me, order):
    n = len(order)
    cols = x.shape[-1] // n
    blocks = [x[..., q * cols:(q + 1) * cols] for q in range(n)]
    bit = 1
    while bit < n:
        take = (me // bit) % 2 == 1
        blocks = [jnp.where(take, blocks[q ^ bit], blocks[q]) for q in range(n)]
        bit *= 2
    return [blocks[m] for m in order]


def gather_parts(parts, bits):
    far = bits[:-1]
    out = []
    early = None
    for turn, part in enumerate(parts):
        axes = list(range(len(far)))
        axes = axes[turn % 2:] + axes[:turn % 2]
        planes = part.shape[0]
        part = part.reshape((planes,) + (1,) * len(bits) + part.shape[1:])
        for at in axes:
            got = swap(part, "expert", far[at])
            early = got if early is None else early
            part = jnp.concatenate([part, got], axis=at + 2)
        part = jnp.concatenate([part, swap(part, "expert", bits[-1])], axis=1)
        out.append(part.reshape(-1, part.shape[-1]))
    return out, early


def plus(a, b):
    return (a.astype(F32) + b.astype(F32)).astype(BF16)


def scatter_sum(x, bits):
    far = bits[:-1]
    x = x.reshape((2,) * len(bits) + x.shape[1:])
    x = plus(x[0], swap(x[1], "expert", bits[-1]))
    cols = x.shape[-1] // 2
    parts = []
    for part, turn in ((x[..., :cols], 0), (x[..., cols:], 1)):
        axes = list(range(len(far)))
        axes = axes[turn:] + axes[:turn]
        for at in axes:
            keep = lax.slice_in_dim(part, 0, 1, axis=at)
            send = lax.slice_in_dim(part, 1, 2, axis=at)
            part = plus(keep, swap(send, "expert", far[at]))
        parts.append(part.reshape(part.shape[-2:]))
    return jnp.concatenate(parts, axis=-1)


def load_weights(place, weight, buffer, sems, blocks, half_index):
    slots, width, hidden = weight.shape
    rows, half = width // blocks, hidden // 2
    copies = []
    for i in range(blocks):
        for s in range(slots):
            copies.append(
                pltpu.make_async_copy(
                    weight.at[
                        s,
                        pl.ds(pl.multiple_of(place[i] * rows, rows), rows),
                        pl.ds(pl.multiple_of(half_index * half, half), half),
                    ],
                    buffer.at[pl.ds(i * rows, rows), pl.ds(s * half, half)],
                    sems.at[i * slots + s],
                )
            )
    for copy in copies:
        copy.start()
    for copy in copies:
        copy.wait()


def hidden_kernel(blocks, experts, place, first, second, weight, *rest):
    act, slope, buffer, sems = rest[-4:]
    slots = weight.shape[0]
    split = first.shape[1]
    width = weight.shape[1]

    @pl.when(pl.program_id(0) == 0)
    def _():
        load_weights(place, weight, buffer, sems, blocks, place[blocks])

    pre = jnp.dot(first[...], buffer[:split], preferred_element_type=F32) + jnp.dot(
        second[:, :width - split], buffer[split:], preferred_element_type=F32
    )
    coefs = second[:, width - split:].astype(F32)
    lane = lax.broadcasted_iota(jnp.int32, coefs.shape, 1)
    half = pre.shape[1] // slots
    for s in range(slots):
        wanted = place[blocks + 1] * slots + s
        named = (lane == wanted) | (lane == wanted + experts)
        coef = jnp.sum(jnp.where(named, coefs, 0.0), axis=1, keepdims=True)
        one = pre[:, s * half:(s + 1) * half]
        sigma = 1.0 / (1.0 + jnp.exp(-one))
        act[:, s * half:(s + 1) * half] = (coef * (one * sigma)).astype(BF16)
        slope[:, s * half:(s + 1) * half] = (coef * (sigma * (1.0 + one * (1.0 - sigma)))).astype(BF16)


def hidden_product(place, parts, weight, experts, total_rows, at_row, filled=None, tile=256):
    first, second = parts
    slots, width, hidden = weight.shape
    blocks = place.shape[0] - 2
    cols = slots * hidden // 2
    rows = first.shape[0]
    skip = at_row // tile
    shape = jax.ShapeDtypeStruct((total_rows, cols), BF16)
    any_space = pl.BlockSpec(memory_space=pl.ANY)
    given = () if filled is None else tuple(filled)
    return pl.pallas_call(
        functools.partial(hidden_kernel, blocks, experts),
        out_shape=[shape, shape],
        grid_spec=pltpu.PrefetchScalarGridSpec(
            num_scalar_prefetch=1,
            grid=(rows // tile,),
            in_specs=[
                pl.BlockSpec((tile, first.shape[1]), lambda i, p: (i, 0)),
                pl.BlockSpec((tile, second.shape[1]), lambda i, p: (i, 0)),
                any_space,
            ]
            + [any_space] * len(given),
            out_specs=[pl.BlockSpec((tile, cols), lambda i, p: (i + skip, 0))] * 2,
            scratch_shapes=[
                pltpu.VMEM((width, cols), BF16),
                pltpu.SemaphoreType.DMA((blocks * slots,)),
            ],
        ),
        input_output_aliases={4: 0, 5: 1} if given else {},
        compiler_params=pltpu.CompilerParams(vmem_limit_bytes=24 * MIB),
        cost_estimate=pl.CostEstimate(
            flops=2 * rows * width * cols,
            bytes_accessed=2 * (rows * width + width * cols + 2 * rows * cols),
            transcendentals=rows * cols,
        ),
        name="hidden_product",
    )(place, first, second, weight, *given)


def back_kernel(blocks, count, place, *refs):
    parts, (weight, slope, out, buffer, sems) = refs[:count], refs[count:]

    @pl.when(pl.program_id(0) == 0)
    def _():
        load_weights(place, weight, buffer, sems, blocks, place[blocks])

    total = None
    at = 0
    for part in parts:
        depth = part.shape[1]
        term = jnp.dot(part[...], buffer[at:at + depth], preferred_element_type=F32)
        total = term if total is None else total + term
        at += depth
    out[...] = (total * slope[...].astype(F32)).astype(BF16)


def back_product(place, parts, weight, slope, tile=256):
    slots, width, hidden = weight.shape
    blocks = place.shape[0] - 2
    cols = slots * hidden // 2
    rows = slope.shape[0]
    return pl.pallas_call(
        functools.partial(back_kernel, blocks, len(parts)),
        out_shape=jax.ShapeDtypeStruct((rows, cols), BF16),
        grid_spec=pltpu.PrefetchScalarGridSpec(
            num_scalar_prefetch=1,
            grid=(rows // tile,),
            in_specs=[pl.BlockSpec((tile, part.shape[1]), lambda i, p: (i, 0)) for part in parts]
            + [pl.BlockSpec(memory_space=pl.ANY), pl.BlockSpec((tile, cols), lambda i, p: (i, 0))],
            out_specs=pl.BlockSpec((tile, cols), lambda i, p: (i, 0)),
            scratch_shapes=[
                pltpu.VMEM((width, cols), BF16),
                pltpu.SemaphoreType.DMA((blocks * slots,)),
            ],
        ),
        compiler_params=pltpu.CompilerParams(vmem_limit_bytes=24 * MIB),
        cost_estimate=pl.CostEstimate(
            flops=2 * rows * width * cols,
            bytes_accessed=2 * (rows * width + width * cols + 2 * rows * cols),
            transcendentals=0,
        ),
        name="back_product",
    )(place, *parts, weight, slope)


def out_kernel(place, own, rest, weight, out, buffer, sems):
    slots, _, hidden = weight.shape
    half = hidden // 2
    rows = out.shape[0]

    @pl.when(pl.program_id(0) == 0)
    def _():
        copies = []
        for s in range(slots):
            for k, (source, index) in enumerate(((own, place[0]), (rest, 1 - place[0]))):
                copies.append(
                    pltpu.make_async_copy(
                        source.at[pl.ds(0, rows), pl.ds(s * half, half)],
                        buffer.at[s, :, pl.ds(pl.multiple_of(index * half, half), half)],
                        sems.at[2 * s + k],
                    )
                )
        for copy in copies:
            copy.start()
        for copy in copies:
            copy.wait()

    total = None
    for s in range(slots):
        term = lax.dot_general(
            buffer[s], weight[s], (((1,), (1,)), ((), ())), preferred_element_type=F32
        )
        total = term if total is None else total + term
    out[...] = total.astype(BF16)


def out_product(half_index, own, rest, weight, tile=256):
    slots, width, hidden = weight.shape
    rows = rest.shape[0]
    return pl.pallas_call(
        out_kernel,
        out_shape=jax.ShapeDtypeStruct((rows, width), BF16),
        grid_spec=pltpu.PrefetchScalarGridSpec(
            num_scalar_prefetch=1,
            grid=(width // tile,),
            in_specs=[
                pl.BlockSpec(memory_space=pl.ANY),
                pl.BlockSpec(memory_space=pl.ANY),
                pl.BlockSpec((slots, tile, hidden), lambda i, p: (0, i, 0)),
            ],
            out_specs=pl.BlockSpec((rows, tile), lambda i, p: (0, i)),
            scratch_shapes=[
                pltpu.VMEM((slots, rows, hidden), BF16),
                pltpu.SemaphoreType.DMA((2 * slots,)),
            ],
        ),
        compiler_params=pltpu.CompilerParams(vmem_limit_bytes=24 * MIB),
        cost_estimate=pl.CostEstimate(
            flops=2 * rows * width * slots * hidden,
            bytes_accessed=2 * (rows * width + width * slots * hidden + rows * slots * hidden),
            transcendentals=0,
        ),
        name="out_product",
    )(half_index, own, rest, weight)


def outer(left, right):
    return lax.dot_general(left, right, (((0,), (0,)), ((), ())), preferred_element_type=F32)


def body(tokens, expert_ids, combine_weight, partner, w_up, w_down, out_grad):
    owners = lax.axis_size("expert")
    groups = lax.axis_size("dp")
    me_g = lax.axis_index("dp")
    me_j = lax.axis_index("expert")
    tok_dev, chosen = expert_ids.shape
    width = tokens.shape[1]
    slots = w_up.shape[1]
    hidden = w_up.shape[2]
    half = hidden // 2
    experts = slots * owners
    rows = width // groups
    top = groups // 2
    upper = me_g // top == 1
    upper_index = (me_g // top).astype(jnp.int32)
    order = block_order(groups)
    bits = [owners >> (i + 1) for i in range(owners.bit_length() - 1)]
    plane = owners * tok_dev
    scale = 1.0 / tok_dev

    named = expert_ids[:, :, None] == jnp.arange(experts, dtype=jnp.int32)[None, None, :]
    coef = jnp.sum(jnp.where(named, combine_weight[:, :, None], 0.0), axis=1)
    coef_hi = lax.reduce_precision(coef, 8, 7)
    coef_lo = coef - coef_hi
    lanes = -(-2 * experts // 128) * 128
    extra = jnp.pad(
        jnp.concatenate([coef_hi, coef_lo], axis=1), ((0, 0), (0, lanes - 2 * experts))
    ).astype(BF16)

    raw = jnp.concatenate([tokens, extra], axis=1)
    other_raw = swap(raw, "dp", top)
    other_grad = swap(after(out_grad, other_raw), "dp", top)

    def token_parts(x):
        blocks = relative_cols(x[:, :width], me_g, order)
        first = jnp.concatenate(blocks[:groups // 2], axis=1)
        second = jnp.concatenate(blocks[groups // 2:] + [x[:, width:]], axis=1)
        return [first[None], second[None]]

    x_own, _ = gather_parts(token_parts(raw), bits)
    x_other, early = gather_parts(token_parts(other_raw), bits)

    pair_grad = jnp.stack([out_grad, other_grad], axis=0)
    blocks = relative_cols(after(pair_grad, early), me_g, order)
    per = groups // 4
    quarters = [jnp.concatenate(blocks[i * per:(i + 1) * per], axis=-1) for i in range(4)]
    g_send, early = gather_parts(quarters[:2], bits)
    g_keep, _ = gather_parts([after(one, early) for one in quarters[2:]], bits)
    g_parts = g_send + g_keep

    up = jnp.swapaxes(w_up, 0, 1)
    down = jnp.swapaxes(w_down, 0, 1)

    offsets = jnp.stack([me_g ^ m for m in order]).astype(jnp.int32)
    me_word = me_j.astype(jnp.int32)

    def place_of(half_index):
        return jnp.concatenate([offsets, half_index[None], me_word[None]])

    place = place_of(upper_index)
    both = hidden_product(place, x_own, up, experts, 2 * plane, 0)
    act, slope = hidden_product(place, x_other, up, experts, 2 * plane, plane, both)

    def down_block(m):
        part, col = divmod(order.index(m) * rows, width // 4)
        return outer(g_parts[part][:, col:col + rows], act) * scale

    def reduced(block_of, split, ahead=None):
        pieces = slots if split else 1
        wide = slots * half // pieces
        cut = lambda x: [x[:, i * wide:(i + 1) * wide] for i in range(pieces)]
        sends = {m: cut(block_of(m).astype(BF16)) for m in order if m & (top - 1)}
        if ahead is not None:
            ahead.append(sends[order[len(sends) - 1]][0])
        kept = {m: block_of(m) for m in (top, 0)}
        kept = {m: cut(x) for m, x in kept.items()}
        own, got = [], []
        for i in range(pieces):
            have = {m: sends[m][i] for m in sends}
            for m in sends:
                bit = m & -m
                piece = swap(have[m], "dp", bit)
                to = m ^ bit
                if to in kept:
                    kept[to][i] = kept[to][i] + piece.astype(F32)
                else:
                    have[to] = plus(have[to], piece)
            own.append(kept[0][i].astype(BF16))
            got.append(swap(kept[top][i].astype(BF16), "dp", top))
        own = own if split else [own[0][:, s * half:(s + 1) * half] for s in range(slots)]
        got = got if split else [got[0][:, s * half:(s + 1) * half] for s in range(slots)]
        return [
            jnp.where(upper, jnp.concatenate([b, a], axis=1), jnp.concatenate([a, b], axis=1))
            for a, b in zip(own, got)
        ]

    def relocated(per_slot):
        first = per_slot[0].reshape(owners, rows // owners, hidden)
        spread = lax.all_to_all(first, "expert", split_axis=0, concat_axis=0, tiled=True)
        moved = lax.all_to_all(spread[partner], "expert", split_axis=0, concat_axis=0, tiled=True)
        return jnp.stack([moved.reshape(rows, hidden)] + per_slot[1:], axis=1)

    down_sent = []
    grad_down = relocated(reduced(down_block, False, down_sent))

    place = place + zero_of(down_sent[0]).astype(jnp.int32)
    pre = back_product(place, g_parts, down, slope)

    def up_block(m):
        part, col = divmod(order.index(m) * rows, width // 2)
        return (
            outer(x_own[part][:, col:col + rows], pre[:plane])
            + outer(x_other[part][:, col:col + rows], pre[plane:])
        ) * scale

    up_sent = []
    grad_up = relocated(reduced(up_block, True, up_sent))

    later = zero_of(up_sent[0]).astype(jnp.int32)
    rest_place = place_of(1 - upper_index) + later
    half_index = upper_index[None] + later
    act_rest, slope_rest = hidden_product(rest_place, x_own, up, experts, plane, 0)
    part_out = out_product(half_index, act, act_rest, down)
    output = scatter_sum(part_out.reshape(owners, tok_dev, width), bits)
    pre_rest = back_product(rest_place, g_parts, down, slope_rest)
    part_in = out_product(half_index, pre, pre_rest, up)
    input_grad = scatter_sum(part_in.reshape(owners, tok_dev, width), bits)
    return (output, input_grad, grad_up, grad_down)


def solution(mesh):
    return jax.shard_map(
        body,
        mesh=mesh,
        in_specs=(
            P(("dp", "expert"), None),
            P(("dp", "expert"), None),
            P(("dp", "expert"), None),
            P(),
            P(None, "expert", None),
            P(None, "expert", None),
            P(("dp", "expert"), None),
        ),
        out_specs=(
            P(("dp", "expert"), None),
            P(("dp", "expert"), None),
            P("dp", "expert", None),
            P("dp", "expert", None),
        ),
        check_vma=False,
    )
```

profile of v0, /device:TPU:0, one launch (start us, length us, event | category | flops | bytes accessed | tf_op | source)
XLA Modules:
  0.0 355.1 jit_solution(17597954075714281332)
XLA Ops:
  3.4 4.0 %collective-permute-start.3 = (bf16[128,2176]{1,0:T(8,128)(2,1)}, bf16[128,2176]{1,0:T(8,128)(2,1)}, u32[]{:S(2)}, u32[]{:S(2)}) collective-permute-start(bf16[128,2176]{1,0:T(8,128)(2,1)} %pad_maximum_fusion.20), channel_id=1, source_target_pairs={{0,16},{8,24},{16,0},{24,8},{1,17},{9,25},{17,1},{25,9},{2,18},{10... | collective-permute-start | bytes 1671176 | tf_op jit(solution)/shard_map/ppermute | solution.py:17
  11.8 6.4 %copy.43 = bf16[2048,2,768]{2,0,1:T(8,128)(2,1)} copy(bf16[2048,2,768]{2,1,0:T(2,128)(2,1)} %param.11) | data formatting | bytes 12582912 | tf_op args[4]
  22.5 9.8 %collective-permute-done.3 = bf16[128,2176]{1,0:T(8,128)(2,1)} collective-permute-done((bf16[128,2176]{1,0:T(8,128)(2,1)}, bf16[128,2176]{1,0:T(8,128)(2,1)}, u32[]{:S(2)}, u32[]{:S(2)}) %collective-permute-start.3) | collective-permute-done | bytes 557088 | tf_op jit(solution)/shard_map/ppermute | solution.py:17
  47.1 14.7 %collective-permute-done.4 = bf16[128,2048]{1,0:T(8,128)(2,1)S(1)} collective-permute-done((bf16[128,2048]{1,0:T(8,128)(2,1)S(1)}, bf16[128,2048]{1,0:T(8,128)(2,1)S(1)}, u32[]{:S(2)}, u32[]{:S(2)}) %collective-permute-start.4) | collective-permute-done | bytes 524320 | tf_op jit(solution)/shard_map/ppermute | solution.py:17
  63.0 9.0 %collective-permute-done.17 = bf16[2,1,1,1,128,512]{5,4,3,2,1,0:T(8,128)(2,1)S(1)} collective-permute-done((bf16[2,1,1,1,128,512]{5,4,3,2,1,0:T(8,128)(2,1)S(1)}, bf16[2,1,1,1,128,512]{5,4,3,2,1,0:T(8,128)(2,1)S(1)}, u32[]{:S(2)}, u32[]{:S(2)}) %collective-permute-start.17) | collective-permute-done | bytes 262176 | tf_op jit(solution)/shard_map/ppermute | solution.py:17
  84.0 5.6 %collective-permute-done.6 = bf16[2,1,1,1,128,512]{5,4,0,3,2,1:T(8,128)(2,1)S(1)} collective-permute-done((bf16[2,1,1,1,128,512]{5,4,0,3,2,1:T(8,128)(2,1)S(1)}, bf16[2,1,1,1,128,512]{5,4,0,3,2,1:T(8,128)(2,1)S(1)}, u32[]{:S(2)}, u32[]{:S(2)}) %collective-permute-start.6) | collective-permute-done | bytes 262176 | tf_op jit(solution)/shard_map/ppermute | solution.py:17
  91.4 9.4 %collective-permute-done.18 = bf16[2,1,2,1,128,512]{5,4,3,2,1,0:T(8,128)(2,1)S(1)} collective-permute-done((bf16[2,1,2,1,128,512]{5,4,3,2,1,0:T(8,128)(2,1)S(1)}, bf16[2,1,2,1,128,512]{5,4,3,2,1,0:T(8,128)(2,1)S(1)}, u32[]{:S(2)}, u32[]{:S(2)}) %collective-permute-start.18) | collective-permute-done | bytes 524320 | tf_op jit(solution)/shard_map/ppermute | solution.py:17
  103.3 5.8 %hidden_product.3 = (bf16[2048,768]{1,0:T(8,128)(2,1)S(1)}, bf16[2048,768]{1,0:T(8,128)(2,1)S(1)}) custom-call(s32[6]{0:T(128)S(1)} %concatenate.181.place, bf16[1024,1024]{1,0:T(8,128)(2,1)S(1)} %bitcast.113, bf16[1024,1152]{1,0:T(8,128)(2,1)S(1)} %bitcast.109, bf16[2,2048,768]{2,1,0:T(8,128)(2,1)S(1)} %bitcast.87), custom_call_target="tpu_custom_call" | custom-call | flops 3221225472 | bytes 10485760 | tf_op jit(solution)/shard_map/hidden_product/pallas_call | solution.py:151
  109.5 5.6 %collective-permute-done.24 = bf16[2,1,1,2,128,512]{5,4,0,3,2,1:T(8,128)(2,1)S(1)} collective-permute-done((bf16[2,1,1,2,128,512]{5,4,0,3,2,1:T(8,128)(2,1)S(1)}, bf16[2,1,1,2,128,512]{5,4,0,3,2,1:T(8,128)(2,1)S(1)}, u32[]{:S(2)}, u32[]{:S(2)}) %collective-permute-start.24) | collective-permute-done | bytes 524320 | tf_op jit(solution)/shard_map/ppermute | solution.py:17
  115.2 5.5 %collective-permute-done.7 = bf16[2,1,1,2,128,512]{5,4,0,3,2,1:T(8,128)(2,1)S(1)} collective-permute-done((bf16[2,1,1,2,128,512]{5,4,0,3,2,1:T(8,128)(2,1)S(1)}, bf16[2,1,1,2,128,512]{5,4,0,3,2,1:T(8,128)(2,1)S(1)}, u32[]{:S(2)}, u32[]{:S(2)}) %collective-permute-start.7) | collective-permute-done | bytes 524320 | tf_op jit(solution)/shard_map/ppermute | solution.py:17
  122.0 5.6 %hidden_product.4 = (bf16[2048,768]{1,0:T(8,128)(2,1)S(1)}, bf16[2048,768]{1,0:T(8,128)(2,1)S(1)}) custom-call(s32[6]{0:T(128)S(1)} %concatenate.181.place, bf16[1024,1024]{1,0:T(8,128)(2,1)S(1)} %bitcast.103, bf16[1024,1152]{1,0:T(8,128)(2,1)S(1)} %bitcast.91, bf16[2,2048,768]{2,1,0:T(8,128)(2,1)S(1)} %bitcast.88, ...), custom_call_target="tpu_custom_call", output_to_operand_aliasing={{0}: (4, {}), {1}: (5, {})} | custom-call | flops 3221225472 | bytes 10485760 | tf_op jit(solution)/shard_map/hidden_product/pallas_call | solution.py:151
  144.1 9.2 %back_product.2.own = bf16[2048,768]{1,0:T(8,128)(2,1)S(1)} custom-call(s32[6]{0:T(128)S(1)} %broadcast_add_fusion.2.place, bf16[2048,512]{1,0:T(8,128)(2,1)S(1)} %bitcast.98, bf16[2048,512]{1,0:T(8,128)(2,1)S(1)} %bitcast.107, bf16[2048,512]{1,0:T(8,128)(2,1)S(1)} %bitcast.101, bf16[2048,512]{1,0:T(8,128)(2,1)S(1)} %bitcast.94, ...), custom_call_target="tpu_custom_call" | custom-call | flops 6442450944 | bytes 17825792 | tf_op jit(solution)/shard_map/back_product/pallas_call | solution.py:202
  169.5 5.6 %hidden_product.5 = (bf16[1024,768]{1,0:T(8,128)(2,1)S(1)}, bf16[1024,768]{1,0:T(8,128)(2,1)S(1)}) custom-call(s32[6]{0:T(128)S(1)} %broadcast_add_fusion.1.place, bf16[1024,1024]{1,0:T(8,128)(2,1)S(1)} %bitcast.116, bf16[1024,1152]{1,0:T(8,128)(2,1)S(1)} %bitcast.111, bf16[2,2048,768]{2,1,0:T(8,128)(2,1)S(1)} %bitcast.89), custom_call_target="tpu_custom_call" | custom-call | flops 3221225472 | bytes 10485760 | tf_op jit(solution)/shard_map/hidden_product/pallas_call | solution.py:151
  175.2 5.0 %back_product.3.rest = bf16[1024,768]{1,0:T(8,128)(2,1)S(1)} custom-call(s32[6]{0:T(128)S(1)} %broadcast_add_fusion.1.place, bf16[2048,512]{1,0:T(8,128)(2,1)S(1)} %bitcast.99, bf16[2048,512]{1,0:T(8,128)(2,1)S(1)} %bitcast.108, bf16[2048,512]{1,0:T(8,128)(2,1)S(1)} %bitcast.102, bf16[2048,512]{1,0:T(8,128)(2,1)S(1)} %bitcast.95, ...), custom_call_target="tpu_custom_call" | custom-call | flops 3221225472 | bytes 10485760 | tf_op jit(solution)/shard_map/back_product/pallas_call | solution.py:202
  180.1 9.4 %out_product.3 = bf16[1024,2048]{1,0:T(8,128)(2,1)S(1)} custom-call(s32[1]{0:T(128)S(6)} %add.132.place, bf16[2048,768]{1,0:T(8,128)(2,1)S(1)} %copy-done.7, bf16[1024,768]{1,0:T(8,128)(2,1)S(1)} %back_product.3.rest, bf16[2,2048,768]{2,1,0:T(8,128)(2,1)S(1)} %bitcast.90), custom_call_target="tpu_custom_call" | custom-call | flops 6442450944 | bytes 13631488 | tf_op jit(solution)/shard_map/out_product/pallas_call | solution.py:260
  192.2 9.8 %out_product.2 = bf16[1024,2048]{1,0:T(8,128)(2,1)S(1)} custom-call(s32[1]{0:T(128)S(6)} %add.132.place, bf16[2048,768]{1,0:T(8,128)(2,1)S(1)} %get-tuple-element.12.own, bf16[1024,768]{1,0:T(8,128)(2,1)S(1)} %get-tuple-element.14.rest, bf16[2,2048,768]{2,1,0:T(8,128)(2,1)S(1)} %bitcast.84), custom_call_target="tpu_custom_call" | custom-call | flops 6442450944 | bytes 13631488 | tf_op jit(solution)/shard_map/out_product/pallas_call | solution.py:260
  215.5 18.6 %collective-permute-done.37 = bf16[512,384]{1,0:T(8,128)(2,1)S(1)} collective-permute-done((bf16[512,384]{1,0:T(8,128)(2,1)S(1)}, bf16[512,384]{1,0:T(8,128)(2,1)S(1)}, u32[]{:S(2)}, u32[]{:S(2)}) %collective-permute-start.37) | collective-permute-done | bytes 393248 | tf_op jit(solution)/shard_map/ppermute | solution.py:17
  235.1 3.5 all-to-all-start
  240.9 3.9 %add_convert_fusion = bf16[512,768]{1,0:T(8,128)(2,1)S(1)} fusion(bf16[512,768]{1,0:T(8,128)(2,1)} %collective-permute-done.44, bf16[2048,512]{1,0:T(8,128)(2,1)S(1)} %bitcast.96, bf16[2048,768]{1,0:T(8,128)(2,1)} %copy-done.2), kind=kOutput, calls=%fused_computation.18 | convolution fusion | flops 1612185600 | bytes 6815744 | tf_op jit(solution)/shard_map/dot_general | solution.py:288
  245.0 19.0 %collective-permute-done.43 = bf16[512,768]{1,0:T(8,128)(2,1)} collective-permute-done((bf16[512,768]{1,0:T(8,128)(2,1)}, bf16[512,768]{1,0:T(8,128)(2,1)}, u32[]{:S(2)}, u32[]{:S(2)}) %collective-permute-start.43) | collective-permute-done | bytes 786464 | tf_op jit(solution)/shard_map/ppermute | solution.py:17
  266.2 4.2 %all-to-all-start.2 = ((bf16[8,64,768]{2,1,0:T(8,128)(2,1)}), bf16[8,64,768]{2,1,0:T(8,128)(2,1)}, u32[]{:S(2)}, u32[]{:S(2)}) async-start(bf16[8,64,768]{2,1,0:T(8,128)(2,1)} %maximum_select_fusion.2), calls=%async_computation.2 | async-start | bytes 1572864 | tf_op jit(solution)/shard_map/all_to_all | solution.py:389
  270.6 20.6 %collective-permute-done.40 = bf16[512,384]{1,0:T(8,128)(2,1)S(1)} collective-permute-done((bf16[512,384]{1,0:T(8,128)(2,1)S(1)}, bf16[512,384]{1,0:T(8,128)(2,1)S(1)}, u32[]{:S(2)}, u32[]{:S(2)}) %collective-permute-start.40) | collective-permute-done | bytes 393248 | tf_op jit(solution)/shard_map/ppermute | solution.py:17
  294.8 4.2 %all-to-all-start.1 = ((bf16[8,64,768]{2,1,0:T(8,128)(2,1)}), bf16[8,64,768]{2,1,0:T(8,128)(2,1)}, u32[]{:S(2)}, u32[]{:S(2)}) async-start(bf16[8,64,768]{2,1,0:T(8,128)(2,1)} %gather_fusion), calls=%async_computation.1 | async-start | bytes 1572864 | tf_op jit(solution)/shard_map/all_to_all | solution.py:390
  314.1 4.4 %all-to-all-start.3 = ((bf16[8,64,768]{2,1,0:T(8,128)(2,1)}), bf16[8,64,768]{2,1,0:T(8,128)(2,1)}, u32[]{:S(2)}, u32[]{:S(2)}) async-start(bf16[8,64,768]{2,1,0:T(8,128)(2,1)} %gather_fusion.1), calls=%async_computation.3 | async-start | bytes 1572864 | tf_op jit(solution)/shard_map/all_to_all | solution.py:390
  (254 shorter events, 151.1 us)
Async XLA Ops:
  3.4 28.9 %collective-permute-start.3 = (bf16[128,2176]{1,0:T(8,128)(2,1)}, bf16[128,2176]{1,0:T(8,128)(2,1)}, u32[]{:S(2)}, u32[]{:S(2)}) collective-permute-start(bf16[128,2176]{1,0:T(8,128)(2,1)} %pad_maximum_fusion.20), channel_id=1, source_target_pairs={{0,16},{8,24},{16,0},{24,8},{1,17},{9,25},{17,1},{25,9},{2,18},{10... | collective-permute-start | bytes 1671176 | tf_op jit(solution)/shard_map/ppermute | solution.py:17
  10.2 29.2 %collective-permute-start.14 = (bf16[1,1,1,1,128,1152]{5,4,3,2,1,0:T(8,128)(2,1)S(1)}, bf16[1,1,1,1,128,1152]{5,4,3,2,1,0:T(8,128)(2,1)S(1)}, u32[]{:S(2)}, u32[]{:S(2)}) collective-permute-start(bf16[1,1,1,1,128,1152]{5,4,3,2,1,0:T(8,128)(2,1)S(1)} %maximum_bitcast_fusion.1), channel_id=1, source_target_pairs={{0,2},{1,3},{2,0},{3,1},{4,6},{5,7},{6,4},{7,5},{8,10},{9,11},{10,... | collective-permute-start | bytes 884744 | tf_op jit(solution)/shard_map/ppermute | solution.py:17
  37.0 24.7 %collective-permute-start.4 = (bf16[128,2048]{1,0:T(8,128)(2,1)S(1)}, bf16[128,2048]{1,0:T(8,128)(2,1)S(1)}, u32[]{:S(2)}, u32[]{:S(2)}) collective-permute-start(bf16[128,2048]{1,0:T(8,128)(2,1)S(1)} %broadcast_add_fusion), channel_id=1, source_target_pairs={{0,16},{8,24},{16,0},{24,8},{1,17},{9,25},{17,1},{25,9},{2,18},{10... | collective-permute-start | bytes 1572872 | tf_op jit(solution)/shard_map/ppermute | solution.py:17
  40.2 49.4 %collective-permute-start.2 = (bf16[1,1,2,2,128,1024]{5,4,3,2,1,0:T(8,128)(2,1)S(1)}, bf16[1,1,2,2,128,1024]{5,4,3,2,1,0:T(8,128)(2,1)S(1)}, u32[]{:S(2)}, u32[]{:S(2)}) collective-permute-start(bf16[1,1,2,2,128,1024]{5,4,3,2,1,0:T(8,128)(2,1)S(1)} %pad_maximum_fusion.12), channel_id=1, source_target_pairs={{0,1},{1,0},{2,3},{3,2},{4,5},{5,4},{6,7},{7,6},{8,9},{9,8},{10,11... | collective-permute-start | bytes 3145736 | tf_op jit(solution)/shard_map/ppermute | solution.py:17
  42.6 32.0 %collective-permute-start.9 = (bf16[1,1,2,1,128,1024]{5,4,3,2,1,0:T(8,128)(2,1)S(1)}, bf16[1,1,2,1,128,1024]{5,4,3,2,1,0:T(8,128)(2,1)S(1)}, u32[]{:S(2)}, u32[]{:S(2)}) collective-permute-start(bf16[1,1,2,1,128,1024]{5,4,3,2,1,0:T(8,128)(2,1)S(1)} %pad_maximum_fusion.23), channel_id=1, source_target_pairs={{0,2},{1,3},{2,0},{3,1},{4,6},{5,7},{6,4},{7,5},{8,10},{9,11},{10,... | collective-permute-start | bytes 1572872 | tf_op jit(solution)/shard_map/ppermute | solution.py:17
  46.5 29.8 %collective-permute-start.12 = (bf16[1,1,1,2,128,1152]{5,4,3,2,1,0:T(8,128)(2,1)S(1)}, bf16[1,1,1,2,128,1152]{5,4,3,2,1,0:T(8,128)(2,1)S(1)}, u32[]{:S(2)}, u32[]{:S(2)}) collective-permute-start(bf16[1,1,1,2,128,1152]{5,4,3,2,1,0:T(8,128)(2,1)S(1)} %pad_maximum_fusion.18), channel_id=1, source_target_pairs={{0,4},{1,5},{2,6},{3,7},{4,0},{5,1},{6,2},{7,3},{8,12},{9,13},{10,... | collective-permute-start | bytes 1769480 | tf_op jit(solution)/shard_map/ppermute | solution.py:17
  62.9 38.8 %collective-permute-start.16 = (bf16[1,1,2,2,128,1152]{5,4,3,2,1,0:T(8,128)(2,1)S(1)}, bf16[1,1,2,2,128,1152]{5,4,3,2,1,0:T(8,128)(2,1)S(1)}, u32[]{:S(2)}, u32[]{:S(2)}) collective-permute-start(bf16[1,1,2,2,128,1152]{5,4,3,2,1,0:T(8,128)(2,1)S(1)} %pad_maximum_fusion.11), channel_id=1, source_target_pairs={{0,1},{1,0},{2,3},{3,2},{4,5},{5,4},{6,7},{7,6},{8,9},{9,8},{10,11... | collective-permute-start | bytes 3538952 | tf_op jit(solution)/shard_map/ppermute | solution.py:17
  83.9 36.9 %collective-permute-start.10 = (bf16[1,1,2,2,128,1024]{5,4,3,2,1,0:T(8,128)(2,1)S(1)}, bf16[1,1,2,2,128,1024]{5,4,3,2,1,0:T(8,128)(2,1)S(1)}, u32[]{:S(2)}, u32[]{:S(2)}) collective-permute-start(bf16[1,1,2,2,128,1024]{5,4,3,2,1,0:T(8,128)(2,1)S(1)} %pad_maximum_fusion.14), channel_id=1, source_target_pairs={{0,1},{1,0},{2,3},{3,2},{4,5},{5,4},{6,7},{7,6},{8,9},{9,8},{10,11... | collective-permute-start | bytes 3145736 | tf_op jit(solution)/shard_map/ppermute | solution.py:17
  89.6 32.1 %collective-permute-start.13 = (bf16[1,1,2,2,128,1152]{5,4,3,2,1,0:T(8,128)(2,1)S(1)}, bf16[1,1,2,2,128,1152]{5,4,3,2,1,0:T(8,128)(2,1)S(1)}, u32[]{:S(2)}, u32[]{:S(2)}) collective-permute-start(bf16[1,1,2,2,128,1152]{5,4,3,2,1,0:T(8,128)(2,1)S(1)} %pad_maximum_fusion.10), channel_id=1, source_target_pairs={{0,1},{1,0},{2,3},{3,2},{4,5},{5,4},{6,7},{7,6},{8,9},{9,8},{10,11... | collective-permute-start | bytes 3538952 | tf_op jit(solution)/shard_map/ppermute | solution.py:17
  132.6 79.8 %collective-permute-start.42 = (bf16[512,768]{1,0:T(8,128)(2,1)}, bf16[512,768]{1,0:T(8,128)(2,1)}, u32[]{:S(2)}, u32[]{:S(2)}) collective-permute-start(bf16[512,768]{1,0:T(8,128)(2,1)} %multiply_convert_fusion), channel_id=1, source_target_pairs={{0,8},{8,0},{16,24},{24,16},{1,9},{9,1},{17,25},{25,17},{2,10},{10... | collective-permute-start | bytes 2359304 | tf_op jit(solution)/shard_map/ppermute | solution.py:17
  160.9 46.3 %collective-permute-start.36 = (bf16[512,384]{1,0:T(8,128)(2,1)}, bf16[512,384]{1,0:T(8,128)(2,1)S(1)}, u32[]{:S(2)}, u32[]{:S(2)}) collective-permute-start(bf16[512,384]{1,0:T(8,128)(2,1)} %get-tuple-element.43), channel_id=1, source_target_pairs={{0,8},{8,0},{16,24},{24,16},{1,9},{9,1},{17,25},{25,17},{2,10},{10... | collective-permute-start | bytes 1179656 | tf_op jit(solution)/shard_map/ppermute | solution.py:17
  160.9 46.5 %collective-permute-start.39 = (bf16[512,384]{1,0:T(8,128)(2,1)}, bf16[512,384]{1,0:T(8,128)(2,1)S(1)}, u32[]{:S(2)}, u32[]{:S(2)}) collective-permute-start(bf16[512,384]{1,0:T(8,128)(2,1)} %get-tuple-element.44), channel_id=1, source_target_pairs={{0,8},{8,0},{16,24},{24,16},{1,9},{9,1},{17,25},{25,17},{2,10},{10... | collective-permute-start | bytes 1179656 | tf_op jit(solution)/shard_map/ppermute | solution.py:17
  165.1 43.4 %collective-permute-start.38 = (bf16[512,384]{1,0:T(8,128)(2,1)}, bf16[512,384]{1,0:T(8,128)(2,1)S(1)}, u32[]{:S(2)}, u32[]{:S(2)}) collective-permute-start(bf16[512,384]{1,0:T(8,128)(2,1)} %get-tuple-element.45), channel_id=1, source_target_pairs={{0,8},{8,0},{16,24},{24,16},{1,9},{9,1},{17,25},{25,17},{2,10},{10... | collective-permute-start | bytes 1179656 | tf_op jit(solution)/shard_map/ppermute | solution.py:17
  165.2 43.7 %collective-permute-start.41 = (bf16[512,384]{1,0:T(8,128)(2,1)S(1)}, bf16[512,384]{1,0:T(8,128)(2,1)S(1)}, u32[]{:S(2)}, u32[]{:S(2)}) collective-permute-start(bf16[512,384]{1,0:T(8,128)(2,1)S(1)} %get-tuple-element.46), channel_id=1, source_target_pairs={{0,8},{8,0},{16,24},{24,16},{1,9},{9,1},{17,25},{25,17},{2,10},{10... | collective-permute-start | bytes 1179656 | tf_op jit(solution)/shard_map/ppermute | solution.py:17
  207.3 33.6 %collective-permute-start.44 = (bf16[512,768]{1,0:T(8,128)(2,1)}, bf16[512,768]{1,0:T(8,128)(2,1)}, u32[]{:S(2)}, u32[]{:S(2)}) collective-permute-start(bf16[512,768]{1,0:T(8,128)(2,1)} %multiply_convert_fusion.3), channel_id=1, source_target_pairs={{0,8},{8,0},{16,24},{24,16},{1,9},{9,1},{17,25},{25,17},{2,10},{10... | collective-permute-start | bytes 2359304 | tf_op jit(solution)/shard_map/ppermute | solution.py:17
  207.4 94.3 %collective-permute-start.31 = (bf16[2,2,128,2048]{3,2,1,0:T(8,128)(2,1)}, bf16[2,2,128,2048]{3,2,1,0:T(8,128)(2,1)}, u32[]{:S(2)}, u32[]{:S(2)}) collective-permute-start(bf16[2,2,128,2048]{3,2,1,0:T(8,128)(2,1)} %bitcast.38), channel_id=1, source_target_pairs={{0,1},{1,0},{2,3},{3,2},{4,5},{5,4},{6,7},{7,6},{8,9},{9,8},{10,11... | collective-permute-start | bytes 6291464 | tf_op jit(solution)/shard_map/ppermute | solution.py:17
  208.5 99.9 %collective-permute-start.26 = (bf16[2,2,128,2048]{3,2,1,0:T(8,128)(2,1)}, bf16[2,2,128,2048]{3,2,1,0:T(8,128)(2,1)}, u32[]{:S(2)}, u32[]{:S(2)}) collective-permute-start(bf16[2,2,128,2048]{3,2,1,0:T(8,128)(2,1)} %bitcast.34), channel_id=1, source_target_pairs={{0,1},{1,0},{2,3},{3,2},{4,5},{5,4},{6,7},{7,6},{8,9},{9,8},{10,11... | collective-permute-start | bytes 6291464 | tf_op jit(solution)/shard_map/ppermute | solution.py:17
  208.9 25.2 %collective-permute-start.37 = (bf16[512,384]{1,0:T(8,128)(2,1)S(1)}, bf16[512,384]{1,0:T(8,128)(2,1)S(1)}, u32[]{:S(2)}, u32[]{:S(2)}) collective-permute-start(bf16[512,384]{1,0:T(8,128)(2,1)S(1)} %get-tuple-element.32), channel_id=1, source_target_pairs={{0,16},{8,24},{16,0},{24,8},{1,17},{9,25},{17,1},{25,9},{2,18},{10... | collective-permute-start | bytes 1179656 | tf_op jit(solution)/shard_map/ppermute | solution.py:17
  214.6 49.3 %collective-permute-start.43 = (bf16[512,768]{1,0:T(8,128)(2,1)}, bf16[512,768]{1,0:T(8,128)(2,1)}, u32[]{:S(2)}, u32[]{:S(2)}) collective-permute-start(bf16[512,768]{1,0:T(8,128)(2,1)} %add_convert_fusion.1), channel_id=1, source_target_pairs={{0,16},{8,24},{16,0},{24,8},{1,17},{9,25},{17,1},{25,9},{2,18},{10... | collective-permute-start | bytes 2359304 | tf_op jit(solution)/shard_map/ppermute | solution.py:17
  235.1 31.1 %all-to-all-start = ((bf16[8,64,768]{2,1,0:T(8,128)(2,1)}), bf16[8,64,768]{2,1,0:T(8,128)(2,1)S(1)}, u32[]{:S(2)}, u32[]{:S(2)}) async-start(bf16[8,64,768]{2,1,0:T(8,128)(2,1)} %maximum_select_fusion), calls=%async_computation | async-start | bytes 1572864 | tf_op jit(solution)/shard_map/all_to_all | solution.py:389
  266.2 28.6 %all-to-all-start.2 = ((bf16[8,64,768]{2,1,0:T(8,128)(2,1)}), bf16[8,64,768]{2,1,0:T(8,128)(2,1)}, u32[]{:S(2)}, u32[]{:S(2)}) async-start(bf16[8,64,768]{2,1,0:T(8,128)(2,1)} %maximum_select_fusion.2), calls=%async_computation.2 | async-start | bytes 1572864 | tf_op jit(solution)/shard_map/all_to_all | solution.py:389
  313.0 24.1 %collective-permute-start.29 = (bf16[2,1,128,1024]{3,2,1,0:T(8,128)(2,1)}, bf16[2,1,128,1024]{3,2,1,0:T(8,128)(2,1)}, u32[]{:S(2)}, u32[]{:S(2)}) collective-permute-start(bf16[2,1,128,1024]{3,2,1,0:T(8,128)(2,1)} %slice.298), channel_id=1, source_target_pairs={{0,2},{1,3},{2,0},{3,1},{4,6},{5,7},{6,4},{7,5},{8,10},{9,11},{10,... | collective-permute-start | bytes 1572872 | tf_op jit(solution)/shard_map/ppermute | solution.py:17
  314.1 29.0 %all-to-all-start.3 = ((bf16[8,64,768]{2,1,0:T(8,128)(2,1)}), bf16[8,64,768]{2,1,0:T(8,128)(2,1)}, u32[]{:S(2)}, u32[]{:S(2)}) async-start(bf16[8,64,768]{2,1,0:T(8,128)(2,1)} %gather_fusion.1), calls=%async_computation.3 | async-start | bytes 1572864 | tf_op jit(solution)/shard_map/all_to_all | solution.py:390
  324.6 23.3 %collective-permute-start.33 = (bf16[1,1,128,1024]{3,2,1,0:T(8,128)(2,1)}, bf16[1,1,128,1024]{3,2,1,0:T(8,128)(2,1)}, u32[]{:S(2)}, u32[]{:S(2)}) collective-permute-start(bf16[1,1,128,1024]{3,2,1,0:T(8,128)(2,1)} %slice.306), channel_id=1, source_target_pairs={{0,2},{1,3},{2,0},{3,1},{4,6},{5,7},{6,4},{7,5},{8,10},{9,11},{10,... | collective-permute-start | bytes 786440 | tf_op jit(solution)/shard_map/ppermute | solution.py:17
  (56 other events, 762.2 us)
where the time goes:
time: 361 us; the launch traced here: 355 us
  waiting for transfers between devices  137 us (38%)
  starting transfers between devices  63.2 us (18%)
  Pallas kernels  50.3 us (14%)
  local copies, waits for them, and re-layouts  42.3 us (12%)
  other arithmetic  35.2 us (10%)
  matrix products  21.8 us (6%)
  between operations  5.15 us (1%)
    ppermute x45, waiting for transfers between devices, swap(): return lax.ppermute(x, axis, [(i, i ^ mask) for i in range(size)])  134 us
    ppermute x45, starting transfers between devices, swap(): return lax.ppermute(x, axis, [(i, i ^ mask) for i in range(size)])  46.9 us
    dot_general x12, matrix products, outer(): lax.dot_general(left, right, (((0,), (0,)), ((), ())), preferred_element_...  21.8 us
    unnamed x66, local copies, waits for them, and re-layouts  19.5 us
    pallas_call x2, Pallas kernels, out_product(): pl.pallas_call(out_kernel, out_shape=jax.ShapeDtypeStruct((rows, width),...  19.2 us
    pallas_call x3, Pallas kernels, hidden_product(): pl.pallas_call(functools.partial(hidden_kernel, blocks, experts), out_sha...  17 us
    pallas_call x2, Pallas kernels, back_product(): pl.pallas_call(functools.partial(back_kernel, blocks, len(parts)), out_sh...  14.1 us
    convert_element_type x6, other arithmetic, plus(): return (a.astype(F32) + b.astype(F32)).astype(BF16)  9.66 us
  transfers between devices with their start and end apart: 49, of which 20 were waited for; matrix products, arithmetic and copies ran while one was open for 26% of the time, Pallas kernels for 14%

commit v1 on v0

--- a/solution.py
+++ b/solution.py
@@ -17,25 +17,28 @@
     return lax.ppermute(x, axis, [(i, i ^ mask) for i in range(size)])
 
 
-def zero_of(x):
-    first = lax.slice(x, (0,) * x.ndim, (1,) * x.ndim).reshape(()).astype(F32)
-    return jnp.minimum(jnp.abs(first), 0.0)
+def nothing_kernel(*refs):
+    del refs
 
 
 def after(x, *given):
-    total = sum(zero_of(one) for one in given)
-    return x + total.astype(x.dtype)
+    any_space = pl.BlockSpec(memory_space=pl.ANY)
+    return pl.pallas_call(
+        nothing_kernel,
+        out_shape=jax.ShapeDtypeStruct(x.shape, x.dtype),
+        in_specs=[any_space] * (1 + len(given)),
+        out_specs=any_space,
+        input_output_aliases={0: 0},
+        cost_estimate=pl.CostEstimate(flops=0, bytes_accessed=0, transcendentals=0),
+        name="after",
+    )(x, *given)
 
 
 def block_order(groups):
     top = groups // 2
-    order = []
-    bit = 1
-    while bit < top:
-        step = [m for m in range(groups) if m & bit and not m & (bit - 1)]
-        order += [m for m in step if m & top] + [m for m in step if not m & top]
-        bit *= 2
-    return order + [top, 0]
+    odd = [m for m in range(top) if m & 1]
+    even = [m for m in range(top - 1, -1, -1) if not m & 1]
+    return [m | top for m in odd] + odd + [m | top for m in even] + even
 
 
 def relative_cols(x, me, order):
@@ -72,21 +75,16 @@
     return (a.astype(F32) + b.astype(F32)).astype(BF16)
 
 
-def scatter_sum(x, bits):
-    far = bits[:-1]
-    x = x.reshape((2,) * len(bits) + x.shape[1:])
-    x = plus(x[0], swap(x[1], "expert", bits[-1]))
-    cols = x.shape[-1] // 2
-    parts = []
-    for part, turn in ((x[..., :cols], 0), (x[..., cols:], 1)):
-        axes = list(range(len(far)))
-        axes = axes[turn:] + axes[:turn]
-        for at in axes:
-            keep = lax.slice_in_dim(part, 0, 1, axis=at)
-            send = lax.slice_in_dim(part, 1, 2, axis=at)
-            part = plus(keep, swap(send, "expert", far[at]))
-        parts.append(part.reshape(part.shape[-2:]))
-    return jnp.concatenate(parts, axis=-1)
+def core_sum(x, bits):
+    x = x.reshape((2, x.shape[0] // 2) + x.shape[1:])
+    return plus(x[0], swap(x[1], "expert", bits[-1]))
+
+
+def far_sum(x, bits):
+    total = x[0].astype(F32)
+    for m in range(1, x.shape[0]):
+        total = total + swap(x[m], "expert", m * 2).astype(F32)
+    return total.astype(BF16)
 
 
 def load_weights(place, weight, buffer, sems, blocks, half_index):
@@ -138,7 +136,7 @@
         slope[:, s * half:(s + 1) * half] = (coef * (sigma * (1.0 + one * (1.0 - sigma)))).astype(BF16)
 
 
-def hidden_product(place, parts, weight, experts, total_rows, at_row, filled=None, tile=256):
+def hidden_product(place, parts, weight, experts, total_rows, at_row, filled=None, given=(), tile=256):
     first, second = parts
     slots, width, hidden = weight.shape
     blocks = place.shape[0] - 2
@@ -147,7 +145,7 @@
     skip = at_row // tile
     shape = jax.ShapeDtypeStruct((total_rows, cols), BF16)
     any_space = pl.BlockSpec(memory_space=pl.ANY)
-    given = () if filled is None else tuple(filled)
+    held = () if filled is None else tuple(filled)
     return pl.pallas_call(
         functools.partial(hidden_kernel, blocks, experts),
         out_shape=[shape, shape],
@@ -159,14 +157,14 @@
                 pl.BlockSpec((tile, second.shape[1]), lambda i, p: (i, 0)),
                 any_space,
             ]
-            + [any_space] * len(given),
+            + [any_space] * (len(held) + len(given)),
             out_specs=[pl.BlockSpec((tile, cols), lambda i, p: (i + skip, 0))] * 2,
             scratch_shapes=[
                 pltpu.VMEM((width, cols), BF16),
                 pltpu.SemaphoreType.DMA((blocks * slots,)),
             ],
         ),
-        input_output_aliases={4: 0, 5: 1} if given else {},
+        input_output_aliases={4: 0, 5: 1} if held else {},
         compiler_params=pltpu.CompilerParams(vmem_limit_bytes=24 * MIB),
         cost_estimate=pl.CostEstimate(
             flops=2 * rows * width * cols,
@@ -174,11 +172,12 @@
             transcendentals=rows * cols,
         ),
         name="hidden_product",
-    )(place, first, second, weight, *given)
+    )(place, first, second, weight, *held, *given)
 
 
 def back_kernel(blocks, count, place, *refs):
-    parts, (weight, slope, out, buffer, sems) = refs[:count], refs[count:]
+    parts, weight, slope = refs[:count], refs[count], refs[count + 1]
+    out, buffer, sems = refs[-3:]
 
     @pl.when(pl.program_id(0) == 0)
     def _():
@@ -194,7 +193,7 @@
     out[...] = (total * slope[...].astype(F32)).astype(BF16)
 
 
-def back_product(place, parts, weight, slope, tile=256):
+def back_product(place, parts, weight, slope, given=(), tile=256):
     slots, width, hidden = weight.shape
     blocks = place.shape[0] - 2
     cols = slots * hidden // 2
@@ -206,7 +205,8 @@
             num_scalar_prefetch=1,
             grid=(rows // tile,),
             in_specs=[pl.BlockSpec((tile, part.shape[1]), lambda i, p: (i, 0)) for part in parts]
-            + [pl.BlockSpec(memory_space=pl.ANY), pl.BlockSpec((tile, cols), lambda i, p: (i, 0))],
+            + [pl.BlockSpec(memory_space=pl.ANY), pl.BlockSpec((tile, cols), lambda i, p: (i, 0))]
+            + [pl.BlockSpec(memory_space=pl.ANY)] * len(given),
             out_specs=pl.BlockSpec((tile, cols), lambda i, p: (i, 0)),
             scratch_shapes=[
                 pltpu.VMEM((width, cols), BF16),
@@ -220,7 +220,7 @@
             transcendentals=0,
         ),
         name="back_product",
-    )(place, *parts, weight, slope)
+    )(place, *parts, weight, slope, *given)
 
 
 def out_kernel(place, own, rest, weight, out, buffer, sems):
@@ -317,25 +317,30 @@
         jnp.concatenate([coef_hi, coef_lo], axis=1), ((0, 0), (0, lanes - 2 * experts))
     ).astype(BF16)
 
-    raw = jnp.concatenate([tokens, extra], axis=1)
-    other_raw = swap(raw, "dp", top)
-    other_grad = swap(after(out_grad, other_raw), "dp", top)
-
-    def token_parts(x):
-        blocks = relative_cols(x[:, :width], me_g, order)
-        first = jnp.concatenate(blocks[:groups // 2], axis=1)
-        second = jnp.concatenate(blocks[groups // 2:] + [x[:, width:]], axis=1)
-        return [first[None], second[None]]
-
-    x_own, _ = gather_parts(token_parts(raw), bits)
-    x_other, early = gather_parts(token_parts(other_raw), bits)
-
-    pair_grad = jnp.stack([out_grad, other_grad], axis=0)
-    blocks = relative_cols(after(pair_grad, early), me_g, order)
-    per = groups // 4
-    quarters = [jnp.concatenate(blocks[i * per:(i + 1) * per], axis=-1) for i in range(4)]
-    g_send, early = gather_parts(quarters[:2], bits)
-    g_keep, _ = gather_parts([after(one, early) for one in quarters[2:]], bits)
+    quarter = groups // 4
+
+    def quarters(x):
+        blocks = relative_cols(x, me_g, order)
+        return [jnp.concatenate(blocks[i * quarter:(i + 1) * quarter], axis=-1) for i in range(4)]
+
+    token_quarters = quarters(tokens)
+    own_first = jnp.concatenate(token_quarters[:2], axis=1)[None]
+    own_second = jnp.concatenate(token_quarters[2:] + [extra], axis=1)[None]
+    x_own, early = gather_parts([own_first, own_second], bits)
+    other_first = swap(own_first, "dp", top)
+    other_second = swap(own_second, "dp", top)
+    x_other, early = gather_parts([other_first, other_second], bits)
+
+    own_grads = quarters(out_grad)
+    got_send = swap(after(jnp.concatenate(own_grads[:2], axis=1), other_first), "dp", top)
+    got_keep = swap(after(jnp.concatenate(own_grads[2:], axis=1), other_second), "dp", top)
+
+    def pair(own, got):
+        cols = own[0].shape[1]
+        return [jnp.stack([own[i], got[:, (1 - i) * cols:(2 - i) * cols]], axis=0) for i in range(2)]
+
+    g_send, early = gather_parts([after(one, early) for one in pair(own_grads[:2], got_send)], bits)
+    g_keep, _ = gather_parts([after(one, early) for one in pair(own_grads[2:], got_keep)], bits)
     g_parts = g_send + g_keep
 
     up = jnp.swapaxes(w_up, 0, 1)
@@ -344,27 +349,26 @@
     offsets = jnp.stack([me_g ^ m for m in order]).astype(jnp.int32)
     me_word = me_j.astype(jnp.int32)
 
-    def place_of(half_index):
-        return jnp.concatenate([offsets, half_index[None], me_word[None]])
+    def place_of(half_index, change=0):
+        return jnp.concatenate([offsets ^ change, half_index[None], me_word[None]])
 
     place = place_of(upper_index)
     both = hidden_product(place, x_own, up, experts, 2 * plane, 0)
-    act, slope = hidden_product(place, x_other, up, experts, 2 * plane, plane, both)
+    act, slope = hidden_product(place_of(upper_index, top), x_other, up, experts, 2 * plane, plane, both)
 
     def down_block(m):
         part, col = divmod(order.index(m) * rows, width // 4)
         return outer(g_parts[part][:, col:col + rows], act) * scale
 
-    def reduced(block_of, split, ahead=None):
-        pieces = slots if split else 1
-        wide = slots * half // pieces
-        cut = lambda x: [x[:, i * wide:(i + 1) * wide] for i in range(pieces)]
-        sends = {m: cut(block_of(m).astype(BF16)) for m in order if m & (top - 1)}
-        if ahead is not None:
-            ahead.append(sends[order[len(sends) - 1]][0])
-        kept = {m: block_of(m) for m in (top, 0)}
-        kept = {m: cut(x) for m, x in kept.items()}
-        own, got = [], []
+    def cut(x, pieces):
+        wide = x.shape[1] // pieces
+        return [x[:, i * wide:(i + 1) * wide] for i in range(pieces)]
+
+    def sent_blocks(block_of, pieces):
+        return {m: cut(block_of(m).astype(BF16), pieces) for m in order if m & (top - 1)}
+
+    def reduced(sends, block_of, pieces, ready):
+        kept = {m: cut(block_of(m), pieces) for m in (top, 0)}
         for i in range(pieces):
             have = {m: sends[m][i] for m in sends}
             for m in sends:
@@ -375,10 +379,14 @@
                     kept[to][i] = kept[to][i] + piece.astype(F32)
                 else:
                     have[to] = plus(have[to], piece)
-            own.append(kept[0][i].astype(BF16))
-            got.append(swap(kept[top][i].astype(BF16), "dp", top))
-        own = own if split else [own[0][:, s * half:(s + 1) * half] for s in range(slots)]
-        got = got if split else [got[0][:, s * half:(s + 1) * half] for s in range(slots)]
+        leaving = [x.astype(BF16) for x in kept[top]]
+        own = [x.astype(BF16) for x in kept[0]]
+        return own, [ready(x) for x in leaving]
+
+    def whole(own, leaving, pieces):
+        got = [swap(x, "dp", top) for x in leaving]
+        if pieces == 1:
+            own, got = cut(own[0], slots), cut(got[0], slots)
         return [
             jnp.where(upper, jnp.concatenate([b, a], axis=1), jnp.concatenate([a, b], axis=1))
             for a, b in zip(own, got)
@@ -390,31 +398,36 @@
         moved = lax.all_to_all(spread[partner], "expert", split_axis=0, concat_axis=0, tiled=True)
         return jnp.stack([moved.reshape(rows, hidden)] + per_slot[1:], axis=1)
 
-    down_sent = []
-    grad_down = relocated(reduced(down_block, False, down_sent))
-
-    place = place + zero_of(down_sent[0]).astype(jnp.int32)
-    pre = back_product(place, g_parts, down, slope)
+    down_sends = sent_blocks(down_block, 1)
+    pre = back_product(place, g_parts, down, slope, given=[x[0] for x in down_sends.values()])
 
     def up_block(m):
         part, col = divmod(order.index(m) * rows, width // 2)
+        other_part, other_col = divmod(order.index(m ^ top) * rows, width // 2)
         return (
             outer(x_own[part][:, col:col + rows], pre[:plane])
-            + outer(x_other[part][:, col:col + rows], pre[plane:])
+            + outer(x_other[other_part][:, other_col:other_col + rows], pre[plane:])
         ) * scale
 
-    up_sent = []
-    grad_up = relocated(reduced(up_block, True, up_sent))
-
-    later = zero_of(up_sent[0]).astype(jnp.int32)
-    rest_place = place_of(1 - upper_index) + later
-    half_index = upper_index[None] + later
-    act_rest, slope_rest = hidden_product(rest_place, x_own, up, experts, plane, 0)
-    part_out = out_product(half_index, act, act_rest, down)
-    output = scatter_sum(part_out.reshape(owners, tok_dev, width), bits)
+    up_sends = sent_blocks(up_block, slots)
+    down_own, down_leaving = reduced(down_sends, down_block, 1, lambda x: x)
+
+    rest_place = place_of(1 - upper_index)
+    act_rest, slope_rest = hidden_product(
+        rest_place, x_own, up, experts, plane, 0, given=down_leaving + [x[-1] for x in up_sends.values()]
+    )
+    part_out = out_product(upper_index[None], act, act_rest, down)
+    out_core = core_sum(part_out.reshape(owners, tok_dev, width), bits)
     pre_rest = back_product(rest_place, g_parts, down, slope_rest)
-    part_in = out_product(half_index, pre, pre_rest, up)
-    input_grad = scatter_sum(part_in.reshape(owners, tok_dev, width), bits)
+    part_in = out_product(upper_index[None], pre, pre_rest, up)
+    in_core = core_sum(part_in.reshape(owners, tok_dev, width), bits)
+
+    up_own, up_leaving = reduced(up_sends, up_block, slots, lambda x: after(x, out_core))
+    up_leaving = up_leaving[:-1] + [after(up_leaving[-1], in_core)]
+    grad_down = relocated(whole(down_own, down_leaving, 1))
+    grad_up = relocated(whole(up_own, up_leaving, slots))
+    output = far_sum(out_core, bits)
+    input_grad = far_sum(in_core, bits)
     return (output, input_grad, grad_up, grad_down)
 
 

time: 361 us -> 337 us (0.934)
  waiting for transfers between devices: 137 us -> 103 us
  other arithmetic: 35.2 us -> 49 us
    ppermute x45, waiting for transfers between devices: 134 us -> 95.1 us  [swap(): return lax.ppermute(x, axis, [(i, i ^ mask) for i in range(size)])]
    concatenate x16, other arithmetic: 1.34 us -> 12.5 us  [gather_parts(): part = jnp.concatenate([part, got], axis=at + 2)]
    slice x20 -> x6, local copies, waits for them, and re-layouts: 17.8 us -> 8.51 us  [the longest x2 5.05 us: core_sum(): return plus(x[0], swap(x[1], 'expert', bits[-1]))]
    convert_element_type x3 -> x5, other arithmetic: 3.38 us -> 10 us  [the longest x2 5.2 us: far_sum(): return total.astype(BF16)]
    unnamed x66 -> x78, local copies, waits for them, and re-layouts: 19.5 us -> 24.8 us
    convert_element_type x6 -> x2, other arithmetic: 9.66 us -> 6.73 us  [plus(): return (a.astype(F32) + b.astype(F32)).astype(BF16)]
  transfers between devices with their start and end apart: 49 -> 49, of which waited for: 20 -> 13; matrix products, arithmetic and copies ran while one was open for 26% -> 29% of each run, Pallas kernels for 14% -> 15%
where the time goes in v1:
time: 337 us; the launch traced here: 330 us
  waiting for transfers between devices  103 us (31%)
  starting transfers between devices  66.1 us (20%)
  Pallas kernels  50.3 us (15%)
  other arithmetic  49 us (15%)
  local copies, waits for them, and re-layouts  40.5 us (12%)
  matrix products  19.1 us (6%)
    ppermute x45, waiting for transfers between devices, swap(): return lax.ppermute(x, axis, [(i, i ^ mask) for i in range(size)])  95.1 us
    ppermute x45, starting transfers between devices, swap(): return lax.ppermute(x, axis, [(i, i ^ mask) for i in range(size)])  50.3 us
    unnamed x78, local copies, waits for them, and re-layouts  24.8 us
    dot_general x12, matrix products, outer(): lax.dot_general(left, right, (((0,), (0,)), ((), ())), preferred_element_...  19.1 us
    pallas_call x2, Pallas kernels, out_product(): pl.pallas_call(out_kernel, out_shape=jax.ShapeDtypeStruct((rows, width),...  18.8 us
    pallas_call x3, Pallas kernels, hidden_product(): pl.pallas_call(functools.partial(hidden_kernel, blocks, experts), out_sha...  17.1 us
    pallas_call x2, Pallas kernels, back_product(): pl.pallas_call(functools.partial(back_kernel, blocks, len(parts)), out_sh...  14.4 us
    concatenate x16, other arithmetic, gather_parts(): part = jnp.concatenate([part, got], axis=at + 2)  12.5 us
  transfers between devices with their start and end apart: 49, of which 13 were waited for; matrix products, arithmetic and copies ran while one was open for 29% of the time, Pallas kernels for 15%

profile of v1, /device:TPU:0, one launch (start us, length us, event | category | flops | bytes accessed | tf_op | source)
XLA Modules:
  0.0 330.2 jit_solution(17305050173451281486)
XLA Ops:
  2.8 4.1 %collective-permute-start.4 = (bf16[1,128,1152]{2,1,0:T(8,128)(2,1)S(1)}, bf16[1,128,1152]{2,1,0:T(8,128)(2,1)}, u32[]{:S(2)}, u32[]{:S(2)}) collective-permute-start(bf16[1,128,1152]{2,1,0:T(8,128)(2,1)S(1)} %get-tuple-element.59), channel_id=1, source_target_pairs={{0,16},{8,24},{16,0},{24,8},{1,17},{9,25},{17,1},{25,9},{2,18},{10... | collective-permute-start | bytes 884744 | tf_op jit(solution)/shard_map/ppermute | solution.py:17
  11.5 6.3 %copy.52 = bf16[2048,2,768]{2,0,1:T(8,128)(2,1)} copy(bf16[2048,2,768]{2,1,0:T(2,128)(2,1)} %param.11) | data formatting | bytes 12582912 | tf_op args[4]
  17.8 6.2 %copy.51 = bf16[2048,2,768]{2,0,1:T(8,128)(2,1)} copy(bf16[2048,2,768]{2,1,0:T(2,128)(2,1)} %param.12) | data formatting | bytes 12582912 | tf_op args[5]
  24.7 6.8 %collective-permute-done.refs_1_ = bf16[1,128,1024]{2,1,0:T(8,128)(2,1)S(1)} collective-permute-done((bf16[1,128,1024]{2,1,0:T(8,128)(2,1)S(1)}, bf16[1,128,1024]{2,1,0:T(8,128)(2,1)S(1)}, u32[]{:S(2)}, u32[]{:S(2)}) %collective-permute-start) | collective-permute-done | bytes 262176 | tf_op jit(solution)/shard_map/ppermute | solution.py:17
  40.5 13.4 %collective-permute-done.15 = bf16[128,1024]{1,0:T(8,128)(2,1)} collective-permute-done((bf16[128,1024]{1,0:T(8,128)(2,1)}, bf16[128,1024]{1,0:T(8,128)(2,1)}, u32[]{:S(2)}, u32[]{:S(2)}) %collective-permute-start.15) | collective-permute-done | bytes 262176 | tf_op jit(solution)/shard_map/ppermute | solution.py:17
  65.0 7.9 %collective-permute-done.16.refs_1_ = bf16[2,1,1,1,128,512]{5,4,3,2,1,0:T(8,128)(2,1)S(1)} collective-permute-done((bf16[2,1,1,1,128,512]{5,4,3,2,1,0:T(8,128)(2,1)}, bf16[2,1,1,1,128,512]{5,4,3,2,1,0:T(8,128)(2,1)S(1)}, u32[]{:S(2)}, u32[]{:S(2)}) %collective-permute-start.16) | collective-permute-done | bytes 262176 | tf_op jit(solution)/shard_map/ppermute | solution.py:17
  83.8 11.1 %collective-permute-done.17 = bf16[2,1,1,1,128,512]{5,4,0,3,2,1:T(8,128)(2,1)S(1)} collective-permute-done((bf16[2,1,1,1,128,512]{5,4,0,3,2,1:T(8,128)(2,1)}, bf16[2,1,1,1,128,512]{5,4,0,3,2,1:T(8,128)(2,1)S(1)}, u32[]{:S(2)}, u32[]{:S(2)}) %collective-permute-start.17) | collective-permute-done | bytes 262176 | tf_op jit(solution)/shard_map/ppermute | solution.py:17
  97.1 6.3 %collective-permute-done.24 = bf16[2,1,1,2,128,512]{5,4,0,3,2,1:T(8,128)(2,1)S(1)} collective-permute-done((bf16[2,1,1,2,128,512]{5,4,0,3,2,1:T(8,128)(2,1)S(1)}, bf16[2,1,1,2,128,512]{5,4,0,3,2,1:T(8,128)(2,1)S(1)}, u32[]{:S(2)}, u32[]{:S(2)}) %collective-permute-start.24) | collective-permute-done | bytes 524320 | tf_op jit(solution)/shard_map/ppermute | solution.py:17
  107.4 5.2 %collective-permute-done.27 = bf16[2,1,1,2,128,512]{5,4,0,3,2,1:T(8,128)(2,1)S(1)} collective-permute-done((bf16[2,1,1,2,128,512]{5,4,0,3,2,1:T(8,128)(2,1)S(1)}, bf16[2,1,1,2,128,512]{5,4,0,3,2,1:T(8,128)(2,1)S(1)}, u32[]{:S(2)}, u32[]{:S(2)}) %collective-permute-start.27) | collective-permute-done | bytes 524320 | tf_op jit(solution)/shard_map/ppermute | solution.py:17
  116.5 5.8 %hidden_product.3 = (bf16[2048,768]{1,0:T(8,128)(2,1)S(1)}, bf16[2048,768]{1,0:T(8,128)(2,1)S(1)}) custom-call(s32[6]{0:T(128)S(1)} %concatenate.181.place, bf16[1024,1024]{1,0:T(8,128)(2,1)S(1)} %bitcast.129, bf16[1024,1152]{1,0:T(8,128)(2,1)S(1)} %bitcast.110, bf16[2,2048,768]{2,1,0:T(8,128)(2,1)S(1)} %bitcast.98), custom_call_target="tpu_custom_call" | custom-call | flops 3221225472 | bytes 10485760 | tf_op jit(solution)/shard_map/hidden_product/pallas_call | solution.py:149
  127.0 5.7 %hidden_product.4 = (bf16[2048,768]{1,0:T(8,128)(2,1)S(1)}, bf16[2048,768]{1,0:T(8,128)(2,1)S(1)}) custom-call(s32[6]{0:T(128)S(1)} %pad_add_fusion.place, bf16[1024,1024]{1,0:T(8,128)(2,1)S(1)} %bitcast.123, bf16[1024,1152]{1,0:T(8,128)(2,1)S(1)} %bitcast.107, bf16[2,2048,768]{2,1,0:T(8,128)(2,1)S(1)} %bitcast.99, ...), custom_call_target="tpu_custom_call", output_to_operand_aliasing={{0}: (4, {}), {1}: (5, {})} | custom-call | flops 3221225472 | bytes 10485760 | tf_op jit(solution)/shard_map/hidden_product/pallas_call | solution.py:149
  143.8 9.2 %back_product.2.own = bf16[2048,768]{1,0:T(8,128)(2,1)S(1)} custom-call(s32[6]{0:T(128)S(1)} %concatenate.181.place, bf16[2048,512]{1,0:T(8,128)(2,1)S(1)} %bitcast.118, bf16[2048,512]{1,0:T(8,128)(2,1)S(1)} %bitcast.115, bf16[2048,512]{1,0:T(8,128)(2,1)S(1)} %bitcast.126, bf16[2048,512]{1,0:T(8,128)(2,1)S(1)} %bitcast.120, ...), custom_call_target="tpu_custom_call" | custom-call | flops 6442450944 | bytes 17825792 | tf_op jit(solution)/shard_map/back_product/pallas_call | solution.py:201
  172.7 5.7 %hidden_product.5 = (bf16[1024,768]{1,0:T(8,128)(2,1)S(1)}, bf16[1024,768]{1,0:T(8,128)(2,1)S(1)}) custom-call(s32[6]{0:T(128)S(1)} %concatenate.188.place, bf16[1024,1024]{1,0:T(8,128)(2,1)S(1)} %bitcast.132, bf16[1024,1152]{1,0:T(8,128)(2,1)S(1)} %bitcast.113, bf16[2,2048,768]{2,1,0:T(8,128)(2,1)S(1)} %bitcast.100, ...), custom_call_target="tpu_custom_call" | custom-call | flops 3221225472 | bytes 10485760 | tf_op jit(solution)/shard_map/hidden_product/pallas_call | solution.py:149
  178.4 5.2 %back_product.3.rest = bf16[1024,768]{1,0:T(8,128)(2,1)S(1)} custom-call(s32[6]{0:T(128)S(1)} %concatenate.188.place, bf16[2048,512]{1,0:T(8,128)(2,1)S(1)} %bitcast.119, bf16[2048,512]{1,0:T(8,128)(2,1)S(1)} %bitcast.116, bf16[2048,512]{1,0:T(8,128)(2,1)S(1)} %bitcast.128, bf16[2048,512]{1,0:T(8,128)(2,1)S(1)} %bitcast.121, ...), custom_call_target="tpu_custom_call" | custom-call | flops 3221225472 | bytes 10485760 | tf_op jit(solution)/shard_map/back_product/pallas_call | solution.py:201
  183.6 9.4 %out_product.2 = bf16[1024,2048]{1,0:T(8,128)(2,1)S(1)} custom-call(s32[1]{0:T(128)} %bitcast.place, bf16[2048,768]{1,0:T(8,128)(2,1)S(1)} %copy-done.5, bf16[1024,768]{1,0:T(8,128)(2,1)S(1)} %get-tuple-element.14.rest, bf16[2,2048,768]{2,1,0:T(8,128)(2,1)S(1)} %bitcast.106), custom_call_target="tpu_custom_call" | custom-call | flops 6442450944 | bytes 13631488 | tf_op jit(solution)/shard_map/out_product/pallas_call | solution.py:260
  195.9 9.4 %out_product.3 = bf16[1024,2048]{1,0:T(8,128)(2,1)S(1)} custom-call(s32[1]{0:T(128)} %bitcast.place, bf16[2048,768]{1,0:T(8,128)(2,1)S(1)} %copy-done.8, bf16[1024,768]{1,0:T(8,128)(2,1)S(1)} %back_product.3.rest, bf16[2,2048,768]{2,1,0:T(8,128)(2,1)S(1)} %bitcast.101), custom_call_target="tpu_custom_call" | custom-call | flops 6442450944 | bytes 13631488 | tf_op jit(solution)/shard_map/out_product/pallas_call | solution.py:260
  216.1 3.5 %all-to-all-start.2 = ((bf16[8,64,768]{2,1,0:T(8,128)(2,1)}), bf16[8,64,768]{2,1,0:T(8,128)(2,1)S(1)}, u32[]{:S(2)}, u32[]{:S(2)}) async-start(bf16[8,64,768]{2,1,0:T(8,128)(2,1)} %maximum_select_fusion.2), calls=%async_computation.2 | async-start | bytes 1572864 | tf_op jit(solution)/shard_map/all_to_all | solution.py:397
  222.2 10.0 %collective-permute-done.37 = bf16[512,384]{1,0:T(8,128)(2,1)} collective-permute-done((bf16[512,384]{1,0:T(8,128)(2,1)}, bf16[512,384]{1,0:T(8,128)(2,1)}, u32[]{:S(2)}, u32[]{:S(2)}) %collective-permute-start.37) | collective-permute-done | bytes 393248 | tf_op jit(solution)/shard_map/ppermute | solution.py:17
  240.4 3.7 %fusion.1.refs_1_ = bf16[4,128,2048]{2,1,0:T(8,128)(2,1)} fusion(bf16[4,128,2048]{2,1,0:T(8,128)(2,1)S(1)} %bitcast.134, bf16[4,128,2048]{2,1,0:T(8,128)(2,1)} %collective-permute-done.29), kind=kLoop, calls=%fused_computation.7 | loop fusion | flops 4194304 | bytes 6291456 | tf_op jit(solution)/shard_map/convert_element_type | solution.py:75
  254.9 19.2 %collective-permute-done.38 = bf16[512,384]{1,0:T(8,128)(2,1)} collective-permute-done((bf16[512,384]{1,0:T(8,128)(2,1)}, bf16[512,384]{1,0:T(8,128)(2,1)}, u32[]{:S(2)}, u32[]{:S(2)}) %collective-permute-start.38) | collective-permute-done | bytes 393248 | tf_op jit(solution)/shard_map/ppermute | solution.py:17
  277.5 4.5 %all-to-all-start = ((bf16[8,64,768]{2,1,0:T(8,128)(2,1)}), bf16[8,64,768]{2,1,0:T(8,128)(2,1)S(1)}, u32[]{:S(2)}, u32[]{:S(2)}) async-start(bf16[8,64,768]{2,1,0:T(8,128)(2,1)} %maximum_select_fusion), calls=%async_computation | async-start | bytes 1572864 | tf_op jit(solution)/shard_map/all_to_all | solution.py:397
  296.5 4.2 %all-to-all-start.1 = ((bf16[8,64,768]{2,1,0:T(8,128)(2,1)}), bf16[8,64,768]{2,1,0:T(8,128)(2,1)}, u32[]{:S(2)}, u32[]{:S(2)}) async-start(bf16[8,64,768]{2,1,0:T(8,128)(2,1)} %gather_fusion), calls=%async_computation.1 | async-start | bytes 1572864 | tf_op jit(solution)/shard_map/all_to_all | solution.py:398
  305.4 12.2 %collective-permute-done.32 = bf16[128,2048]{1,0:T(8,128)(2,1)} collective-permute-done((bf16[128,2048]{1,0:T(8,128)(2,1)}, bf16[128,2048]{1,0:T(8,128)(2,1)}, u32[]{:S(2)}, u32[]{:S(2)}) %collective-permute-start.32) | collective-permute-done | bytes 524320 | tf_op jit(solution)/shard_map/ppermute | solution.py:17
  320.1 5.5 %all-to-all-done.1 = bf16[8,64,768]{2,1,0:T(8,128)(2,1)} async-done(((bf16[8,64,768]{2,1,0:T(8,128)(2,1)}), bf16[8,64,768]{2,1,0:T(8,128)(2,1)}, u32[]{:S(2)}, u32[]{:S(2)}) %all-to-all-start.1) | async-done | bytes 786464 | tf_op jit(solution)/shard_map/all_to_all | solution.py:398
  (252 shorter events, 147.7 us)
Async XLA Ops:
  2.8 33.3 %collective-permute-start.4 = (bf16[1,128,1152]{2,1,0:T(8,128)(2,1)S(1)}, bf16[1,128,1152]{2,1,0:T(8,128)(2,1)}, u32[]{:S(2)}, u32[]{:S(2)}) collective-permute-start(bf16[1,128,1152]{2,1,0:T(8,128)(2,1)S(1)} %get-tuple-element.59), channel_id=1, source_target_pairs={{0,16},{8,24},{16,0},{24,8},{1,17},{9,25},{17,1},{25,9},{2,18},{10... | collective-permute-start | bytes 884744 | tf_op jit(solution)/shard_map/ppermute | solution.py:17
  6.9 29.8 %collective-permute-start.11 = (bf16[1,1,1,1,128,1152]{5,4,3,2,1,0:T(8,128)(2,1)S(1)}, bf16[1,1,1,1,128,1152]{5,4,3,2,1,0:T(8,128)(2,1)S(1)}, u32[]{:S(2)}, u32[]{:S(2)}) collective-permute-start(bf16[1,1,1,1,128,1152]{5,4,3,2,1,0:T(8,128)(2,1)S(1)} %get-tuple-element.58), channel_id=1, source_target_pairs={{0,2},{1,3},{2,0},{3,1},{4,6},{5,7},{6,4},{7,5},{8,10},{9,11},{10,... | collective-permute-start | bytes 884744 | tf_op jit(solution)/shard_map/ppermute | solution.py:17
  32.2 25.1 %collective-permute-start.1 = (bf16[1,1,1,1,128,1024]{5,4,3,2,1,0:T(8,128)(2,1)}, bf16[1,1,1,1,128,1024]{5,4,3,2,1,0:T(8,128)(2,1)S(1)}, u32[]{:S(2)}, u32[]{:S(2)}) collective-permute-start(bf16[1,1,1,1,128,1024]{5,4,3,2,1,0:T(8,128)(2,1)} %bitcast.151), channel_id=1, source_target_pairs={{0,4},{1,5},{2,6},{3,7},{4,0},{5,1},{6,2},{7,3},{8,12},{9,13},{10,... | collective-permute-start | bytes 786440 | tf_op jit(solution)/shard_map/ppermute | solution.py:17
  34.6 42.7 %collective-permute-start.9 = (bf16[1,1,2,1,128,1024]{5,4,3,2,1,0:T(8,128)(2,1)}, bf16[1,1,2,1,128,1024]{5,4,3,2,1,0:T(8,128)(2,1)}, u32[]{:S(2)}, u32[]{:S(2)}) collective-permute-start(bf16[1,1,2,1,128,1024]{5,4,3,2,1,0:T(8,128)(2,1)} %pad_maximum_fusion.21), channel_id=1, source_target_pairs={{0,2},{1,3},{2,0},{3,1},{4,6},{5,7},{6,4},{7,5},{8,10},{9,11},{10,... | collective-permute-start | bytes 1572872 | tf_op jit(solution)/shard_map/ppermute | solution.py:17
  36.1 26.5 %collective-permute-start.5 = (bf16[1,1,1,1,128,1152]{5,4,3,2,1,0:T(8,128)(2,1)}, bf16[1,1,1,1,128,1152]{5,4,3,2,1,0:T(8,128)(2,1)S(1)}, u32[]{:S(2)}, u32[]{:S(2)}) collective-permute-start(bf16[1,1,1,1,128,1152]{5,4,3,2,1,0:T(8,128)(2,1)} %bitcast.10), channel_id=1, source_target_pairs={{0,2},{1,3},{2,0},{3,1},{4,6},{5,7},{6,4},{7,5},{8,10},{9,11},{10,... | collective-permute-start | bytes 884744 | tf_op jit(solution)/shard_map/ppermute | solution.py:17
  53.9 26.2 %collective-permute-start.12 = (bf16[1,1,1,2,128,1152]{5,4,3,2,1,0:T(8,128)(2,1)}, bf16[1,1,1,2,128,1152]{5,4,3,2,1,0:T(8,128)(2,1)S(1)}, u32[]{:S(2)}, u32[]{:S(2)}) collective-permute-start(bf16[1,1,1,2,128,1152]{5,4,3,2,1,0:T(8,128)(2,1)} %pad_maximum_fusion.19), channel_id=1, source_target_pairs={{0,4},{1,5},{2,6},{3,7},{4,0},{5,1},{6,2},{7,3},{8,12},{9,13},{10,... | collective-permute-start | bytes 1769480 | tf_op jit(solution)/shard_map/ppermute | solution.py:17
  81.6 31.8 %collective-permute-start.10 = (bf16[1,1,2,2,128,1024]{5,4,3,2,1,0:T(8,128)(2,1)S(1)}, bf16[1,1,2,2,128,1024]{5,4,3,2,1,0:T(8,128)(2,1)S(1)}, u32[]{:S(2)}, u32[]{:S(2)}) collective-permute-start(bf16[1,1,2,2,128,1024]{5,4,3,2,1,0:T(8,128)(2,1)S(1)} %pad_maximum_fusion.13), channel_id=1, source_target_pairs={{0,1},{1,0},{2,3},{3,2},{4,5},{5,4},{6,7},{7,6},{8,9},{9,8},{10,11... | collective-permute-start | bytes 3145736 | tf_op jit(solution)/shard_map/ppermute | solution.py:17
  83.8 31.5 %collective-permute-start.13 = (bf16[1,1,2,2,128,1152]{5,4,3,2,1,0:T(8,128)(2,1)S(1)}, bf16[1,1,2,2,128,1152]{5,4,3,2,1,0:T(8,128)(2,1)S(1)}, u32[]{:S(2)}, u32[]{:S(2)}) collective-permute-start(bf16[1,1,2,2,128,1152]{5,4,3,2,1,0:T(8,128)(2,1)S(1)} %pad_maximum_fusion.11), channel_id=1, source_target_pairs={{0,1},{1,0},{2,3},{3,2},{4,5},{5,4},{6,7},{7,6},{8,9},{9,8},{10,11... | collective-permute-start | bytes 3538952 | tf_op jit(solution)/shard_map/ppermute | solution.py:17
  134.6 34.4 %collective-permute-start.22 = (bf16[512,768]{1,0:T(8,128)(2,1)S(1)}, bf16[512,768]{1,0:T(8,128)(2,1)S(1)}, u32[]{:S(2)}, u32[]{:S(2)}) collective-permute-start(bf16[512,768]{1,0:T(8,128)(2,1)S(1)} %multiply_convert_fusion.3.refs_6_), channel_id=1, source_target_pairs={{0,8},{8,0},{16,24},{24,16},{1,9},{9,1},{17,25},{25,17},{2,10},{10... | collective-permute-start | bytes 2359304 | tf_op jit(solution)/shard_map/ppermute | solution.py:17
  139.9 67.9 %collective-permute-start.44 = (bf16[512,768]{1,0:T(8,128)(2,1)}, bf16[512,768]{1,0:T(8,128)(2,1)}, u32[]{:S(2)}, u32[]{:S(2)}) collective-permute-start(bf16[512,768]{1,0:T(8,128)(2,1)} %multiply_convert_fusion.2.refs_7_), channel_id=1, source_target_pairs={{0,8},{8,0},{16,24},{24,16},{1,9},{9,1},{17,25},{25,17},{2,10},{10... | collective-permute-start | bytes 2359304 | tf_op jit(solution)/shard_map/ppermute | solution.py:17
  160.8 54.2 %collective-permute-start.39 = (bf16[512,384]{1,0:T(8,128)(2,1)S(1)}, bf16[512,384]{1,0:T(8,128)(2,1)S(1)}, u32[]{:S(2)}, u32[]{:S(2)}) collective-permute-start(bf16[512,384]{1,0:T(8,128)(2,1)S(1)} %get-tuple-element.48), channel_id=1, source_target_pairs={{0,8},{8,0},{16,24},{24,16},{1,9},{9,1},{17,25},{25,17},{2,10},{10... | collective-permute-start | bytes 1179656 | tf_op jit(solution)/shard_map/ppermute | solution.py:17
  162.8 56.9 %collective-permute-start.42 = (bf16[512,384]{1,0:T(8,128)(2,1)}, bf16[512,384]{1,0:T(8,128)(2,1)}, u32[]{:S(2)}, u32[]{:S(2)}) collective-permute-start(bf16[512,384]{1,0:T(8,128)(2,1)} %get-tuple-element.49.rest_2_), channel_id=1, source_target_pairs={{0,8},{8,0},{16,24},{24,16},{1,9},{9,1},{17,25},{25,17},{2,10},{10... | collective-permute-start | bytes 1179656 | tf_op jit(solution)/shard_map/ppermute | solution.py:17
  169.2 43.0 %collective-permute-start.43 = (bf16[512,768]{1,0:T(8,128)(2,1)S(1)}, bf16[512,768]{1,0:T(8,128)(2,1)S(1)}, u32[]{:S(2)}, u32[]{:S(2)}) collective-permute-start(bf16[512,768]{1,0:T(8,128)(2,1)S(1)} %add_convert_fusion.1.rest_0_), channel_id=1, source_target_pairs={{0,16},{8,24},{16,0},{24,8},{1,17},{9,25},{17,1},{25,9},{2,18},{10... | collective-permute-start | bytes 2359304 | tf_op jit(solution)/shard_map/ppermute | solution.py:17
  205.2 35.2 %collective-permute-start.29 = (bf16[4,128,2048]{2,1,0:T(8,128)(2,1)}, bf16[4,128,2048]{2,1,0:T(8,128)(2,1)}, u32[]{:S(2)}, u32[]{:S(2)}) collective-permute-start(bf16[4,128,2048]{2,1,0:T(8,128)(2,1)} %bitcast.36), channel_id=1, source_target_pairs={{0,1},{1,0},{2,3},{3,2},{4,5},{5,4},{6,7},{7,6},{8,9},{9,8},{10,11... | collective-permute-start | bytes 6291464 | tf_op jit(solution)/shard_map/ppermute | solution.py:17
  207.8 36.4 %collective-permute-start.33 = (bf16[4,128,2048]{2,1,0:T(8,128)(2,1)}, bf16[4,128,2048]{2,1,0:T(8,128)(2,1)}, u32[]{:S(2)}, u32[]{:S(2)}) collective-permute-start(bf16[4,128,2048]{2,1,0:T(8,128)(2,1)} %bitcast.42), channel_id=1, source_target_pairs={{0,1},{1,0},{2,3},{3,2},{4,5},{5,4},{6,7},{7,6},{8,9},{9,8},{10,11... | collective-permute-start | bytes 6291464 | tf_op jit(solution)/shard_map/ppermute | solution.py:17
  236.8 39.7 %all-to-all-start.3 = ((bf16[8,64,768]{2,1,0:T(8,128)(2,1)}), bf16[8,64,768]{2,1,0:T(8,128)(2,1)S(1)}, u32[]{:S(2)}, u32[]{:S(2)}) async-start(bf16[8,64,768]{2,1,0:T(8,128)(2,1)} %gather_fusion.1), calls=%async_computation.3 | async-start | bytes 1572864 | tf_op jit(solution)/shard_map/all_to_all | solution.py:398
  244.1 30.0 %collective-permute-start.38 = (bf16[512,384]{1,0:T(8,128)(2,1)}, bf16[512,384]{1,0:T(8,128)(2,1)}, u32[]{:S(2)}, u32[]{:S(2)}) collective-permute-start(bf16[512,384]{1,0:T(8,128)(2,1)} %after.15), channel_id=1, source_target_pairs={{0,16},{8,24},{16,0},{24,8},{1,17},{9,25},{17,1},{25,9},{2,18},{10... | collective-permute-start | bytes 1179656 | tf_op jit(solution)/shard_map/ppermute | solution.py:17
  248.5 41.2 %collective-permute-start.34 = (bf16[128,2048]{1,0:T(8,128)(2,1)}, bf16[128,2048]{1,0:T(8,128)(2,1)}, u32[]{:S(2)}, u32[]{:S(2)}) collective-permute-start(bf16[128,2048]{1,0:T(8,128)(2,1)} %get-tuple-element.32), channel_id=1, source_target_pairs={{0,2},{1,3},{2,0},{3,1},{4,6},{5,7},{6,4},{7,5},{8,10},{9,11},{10,... | collective-permute-start | bytes 1572872 | tf_op jit(solution)/shard_map/ppermute | solution.py:17
  250.4 50.3 %collective-permute-start.36 = (bf16[128,2048]{1,0:T(8,128)(2,1)}, bf16[128,2048]{1,0:T(8,128)(2,1)}, u32[]{:S(2)}, u32[]{:S(2)}) collective-permute-start(bf16[128,2048]{1,0:T(8,128)(2,1)} %get-tuple-element.33), channel_id=1, source_target_pairs={{0,6},{1,7},{2,4},{3,5},{4,2},{5,3},{6,0},{7,1},{8,14},{9,15},{10,... | collective-permute-start | bytes 1572872 | tf_op jit(solution)/shard_map/ppermute | solution.py:17
  251.9 48.8 %collective-permute-start.35 = (bf16[128,2048]{1,0:T(8,128)(2,1)}, bf16[128,2048]{1,0:T(8,128)(2,1)}, u32[]{:S(2)}, u32[]{:S(2)}) collective-permute-start(bf16[128,2048]{1,0:T(8,128)(2,1)} %get-tuple-element.34), channel_id=1, source_target_pairs={{0,4},{1,5},{2,6},{3,7},{4,0},{5,1},{6,2},{7,3},{8,12},{9,13},{10,... | collective-permute-start | bytes 1572872 | tf_op jit(solution)/shard_map/ppermute | solution.py:17
  252.0 36.1 %collective-permute-start.41 = (bf16[512,384]{1,0:T(8,128)(2,1)}, bf16[512,384]{1,0:T(8,128)(2,1)}, u32[]{:S(2)}, u32[]{:S(2)}) collective-permute-start(bf16[512,384]{1,0:T(8,128)(2,1)} %after.17), channel_id=1, source_target_pairs={{0,16},{8,24},{16,0},{24,8},{1,17},{9,25},{17,1},{25,9},{2,18},{10... | collective-permute-start | bytes 1179656 | tf_op jit(solution)/shard_map/ppermute | solution.py:17
  288.1 29.5 %collective-permute-start.32 = (bf16[128,2048]{1,0:T(8,128)(2,1)}, bf16[128,2048]{1,0:T(8,128)(2,1)}, u32[]{:S(2)}, u32[]{:S(2)}) collective-permute-start(bf16[128,2048]{1,0:T(8,128)(2,1)} %get-tuple-element.36), channel_id=1, source_target_pairs={{0,6},{1,7},{2,4},{3,5},{4,2},{5,3},{6,0},{7,1},{8,14},{9,15},{10,... | collective-permute-start | bytes 1572872 | tf_op jit(solution)/shard_map/ppermute | solution.py:17
  289.7 27.9 %collective-permute-start.31 = (bf16[128,2048]{1,0:T(8,128)(2,1)}, bf16[128,2048]{1,0:T(8,128)(2,1)}, u32[]{:S(2)}, u32[]{:S(2)}) collective-permute-start(bf16[128,2048]{1,0:T(8,128)(2,1)} %get-tuple-element.37), channel_id=1, source_target_pairs={{0,4},{1,5},{2,6},{3,7},{4,0},{5,1},{6,2},{7,3},{8,12},{9,13},{10,... | collective-permute-start | bytes 1572872 | tf_op jit(solution)/shard_map/ppermute | solution.py:17
  296.5 29.2 %all-to-all-start.1 = ((bf16[8,64,768]{2,1,0:T(8,128)(2,1)}), bf16[8,64,768]{2,1,0:T(8,128)(2,1)}, u32[]{:S(2)}, u32[]{:S(2)}) async-start(bf16[8,64,768]{2,1,0:T(8,128)(2,1)} %gather_fusion), calls=%async_computation.1 | async-start | bytes 1572864 | tf_op jit(solution)/shard_map/all_to_all | solution.py:398
  (62 other events, 733.7 us)

commit v2 on v1

--- a/solution.py
+++ b/solution.py
@@ -165,7 +165,7 @@
             ],
         ),
         input_output_aliases={4: 0, 5: 1} if held else {},
-        compiler_params=pltpu.CompilerParams(vmem_limit_bytes=24 * MIB),
+        compiler_params=pltpu.CompilerParams(vmem_limit_bytes=16 * MIB),
         cost_estimate=pl.CostEstimate(
             flops=2 * rows * width * cols,
             bytes_accessed=2 * (rows * width + width * cols + 2 * rows * cols),
@@ -213,7 +213,7 @@
                 pltpu.SemaphoreType.DMA((blocks * slots,)),
             ],
         ),
-        compiler_params=pltpu.CompilerParams(vmem_limit_bytes=24 * MIB),
+        compiler_params=pltpu.CompilerParams(vmem_limit_bytes=16 * MIB),
         cost_estimate=pl.CostEstimate(
             flops=2 * rows * width * cols,
             bytes_accessed=2 * (rows * width + width * cols + 2 * rows * cols),
@@ -274,7 +274,7 @@
                 pltpu.SemaphoreType.DMA((2 * slots,)),
             ],
         ),
-        compiler_params=pltpu.CompilerParams(vmem_limit_bytes=24 * MIB),
+        compiler_params=pltpu.CompilerParams(vmem_limit_bytes=16 * MIB),
         cost_estimate=pl.CostEstimate(
             flops=2 * rows * width * slots * hidden,
             bytes_accessed=2 * (rows * width + width * slots * hidden + rows * slots * hidden),
@@ -329,11 +329,11 @@
     x_own, early = gather_parts([own_first, own_second], bits)
     other_first = swap(own_first, "dp", top)
     other_second = swap(own_second, "dp", top)
-    x_other, early = gather_parts([other_first, other_second], bits)
+    x_other, early = gather_parts([after(other_first, early), after(other_second, early)], bits)
 
     own_grads = quarters(out_grad)
     got_send = swap(after(jnp.concatenate(own_grads[:2], axis=1), other_first), "dp", top)
-    got_keep = swap(after(jnp.concatenate(own_grads[2:], axis=1), other_second), "dp", top)
+    got_keep = swap(after(jnp.concatenate(own_grads[2:], axis=1), got_send), "dp", top)
 
     def pair(own, got):
         cols = own[0].shape[1]

time: 337 us -> 329 us (0.976)
  waiting for transfers between devices: 103 us -> 96.1 us
  starting transfers between devices: 66.1 us -> 59.9 us
    ppermute x45, waiting for transfers between devices: 95.1 us -> 87.9 us  [swap(): return lax.ppermute(x, axis, [(i, i ^ mask) for i in range(size)])]
    ppermute x45, starting transfers between devices: 50.3 us -> 43.4 us  [swap(): return lax.ppermute(x, axis, [(i, i ^ mask) for i in range(size)])]
    unnamed x78 -> x74, local copies, waits for them, and re-layouts: 24.8 us -> 24.4 us
  transfers between devices with their start and end apart: 49 -> 49, of which waited for: 13 -> 16; matrix products, arithmetic and copies ran while one was open for 29% -> 31% of each run, Pallas kernels for 15% -> 16%
where the time goes in v2:
time: 329 us; the launch traced here: 322 us
  waiting for transfers between devices  96.1 us (29%)
  starting transfers between devices  59.9 us (18%)
  other arithmetic  52.2 us (16%)
  Pallas kernels  50.4 us (15%)
  local copies, waits for them, and re-layouts  41.1 us (12%)
  matrix products  20.4 us (6%)
    ppermute x45, waiting for transfers between devices, swap(): return lax.ppermute(x, axis, [(i, i ^ mask) for i in range(size)])  87.9 us
    ppermute x45, starting transfers between devices, swap(): return lax.ppermute(x, axis, [(i, i ^ mask) for i in range(size)])  43.4 us
    unnamed x74, local copies, waits for them, and re-layouts  24.4 us
    dot_general x12, matrix products, outer(): lax.dot_general(left, right, (((0,), (0,)), ((), ())), preferred_element_...  20.4 us
    pallas_call x2, Pallas kernels, out_product(): pl.pallas_call(out_kernel, out_shape=jax.ShapeDtypeStruct((rows, width),...  18.8 us
    pallas_call x3, Pallas kernels, hidden_product(): pl.pallas_call(functools.partial(hidden_kernel, blocks, experts), out_sha...  17.2 us
    pallas_call x2, Pallas kernels, back_product(): pl.pallas_call(functools.partial(back_kernel, blocks, len(parts)), out_sh...  14.5 us
    concatenate x16, other arithmetic, gather_parts(): part = jnp.concatenate([part, got], axis=at + 2)  12.5 us
  transfers between devices with their start and end apart: 49, of which 16 were waited for; matrix products, arithmetic and copies ran while one was open for 31% of the time, Pallas kernels for 16%

profile of v2, /device:TPU:0, one launch (start us, length us, event | category | flops | bytes accessed | tf_op | source)
XLA Modules:
  0.0 322.0 jit_solution(17335609960231329197)
XLA Ops:
  2.8 4.1 %collective-permute-start.5 = (bf16[1,128,1152]{2,1,0:T(8,128)(2,1)S(1)}, bf16[1,128,1152]{2,1,0:T(8,128)(2,1)S(1)}, u32[]{:S(2)}, u32[]{:S(2)}) collective-permute-start(bf16[1,128,1152]{2,1,0:T(8,128)(2,1)S(1)} %get-tuple-element.59), channel_id=1, source_target_pairs={{0,16},{8,24},{16,0},{24,8},{1,17},{9,25},{17,1},{25,9},{2,18},{10... | collective-permute-start | bytes 884744 | tf_op jit(solution)/shard_map/ppermute | solution.py:17
  11.5 6.3 %copy.54 = bf16[2048,2,768]{2,0,1:T(8,128)(2,1)} copy(bf16[2048,2,768]{2,1,0:T(2,128)(2,1)} %param.11) | data formatting | bytes 12582912 | tf_op args[4]
  17.8 6.2 %copy.53 = bf16[2048,2,768]{2,0,1:T(8,128)(2,1)} copy(bf16[2048,2,768]{2,1,0:T(2,128)(2,1)} %param.12) | data formatting | bytes 12582912 | tf_op args[5]
  24.7 6.8 %collective-permute-done.refs_0_.refs_1_ = bf16[1,128,1024]{2,1,0:T(8,128)(2,1)S(1)} collective-permute-done((bf16[1,128,1024]{2,1,0:T(8,128)(2,1)S(1)}, bf16[1,128,1024]{2,1,0:T(8,128)(2,1)S(1)}, u32[]{:S(2)}, u32[]{:S(2)}) %collective-permute-start) | collective-permute-done | bytes 262176 | tf_op jit(solution)/shard_map/ppermute | solution.py:17
  40.3 6.1 %collective-permute-done.14.refs_1_ = bf16[128,1024]{1,0:T(8,128)(2,1)S(1)} collective-permute-done((bf16[128,1024]{1,0:T(8,128)(2,1)}, bf16[128,1024]{1,0:T(8,128)(2,1)S(1)}, u32[]{:S(2)}, u32[]{:S(2)}) %collective-permute-start.14) | collective-permute-done | bytes 262176 | tf_op jit(solution)/shard_map/ppermute | solution.py:17
  71.1 4.6 %collective-permute-done.3 = bf16[1,1,2,1,128,1024]{5,4,3,2,1,0:T(8,128)(2,1)} collective-permute-done((bf16[1,1,2,1,128,1024]{5,4,3,2,1,0:T(8,128)(2,1)}, bf16[1,1,2,1,128,1024]{5,4,3,2,1,0:T(8,128)(2,1)}, u32[]{:S(2)}, u32[]{:S(2)}) %collective-permute-start.3) | collective-permute-done | bytes 524320 | tf_op jit(solution)/shard_map/ppermute | solution.py:17
  80.1 5.4 %collective-permute-done.17 = bf16[2,1,1,1,128,512]{5,4,0,3,2,1:T(8,128)(2,1)S(1)} collective-permute-done((bf16[2,1,1,1,128,512]{5,4,0,3,2,1:T(8,128)(2,1)}, bf16[2,1,1,1,128,512]{5,4,0,3,2,1:T(8,128)(2,1)S(1)}, u32[]{:S(2)}, u32[]{:S(2)}) %collective-permute-start.17) | collective-permute-done | bytes 262176 | tf_op jit(solution)/shard_map/ppermute | solution.py:17
  87.6 7.2 %collective-permute-done.24 = bf16[2,1,1,2,128,512]{5,4,0,3,2,1:T(8,128)(2,1)S(1)} collective-permute-done((bf16[2,1,1,2,128,512]{5,4,0,3,2,1:T(8,128)(2,1)S(1)}, bf16[2,1,1,2,128,512]{5,4,0,3,2,1:T(8,128)(2,1)S(1)}, u32[]{:S(2)}, u32[]{:S(2)}) %collective-permute-start.24) | collective-permute-done | bytes 524320 | tf_op jit(solution)/shard_map/ppermute | solution.py:17
  100.4 6.5 %collective-permute-done.27 = bf16[2,1,1,2,128,512]{5,4,0,3,2,1:T(8,128)(2,1)S(1)} collective-permute-done((bf16[2,1,1,2,128,512]{5,4,0,3,2,1:T(8,128)(2,1)S(1)}, bf16[2,1,1,2,128,512]{5,4,0,3,2,1:T(8,128)(2,1)S(1)}, u32[]{:S(2)}, u32[]{:S(2)}) %collective-permute-start.27) | collective-permute-done | bytes 524320 | tf_op jit(solution)/shard_map/ppermute | solution.py:17
  110.4 5.8 %hidden_product.3 = (bf16[2048,768]{1,0:T(8,128)(2,1)S(1)}, bf16[2048,768]{1,0:T(8,128)(2,1)S(1)}) custom-call(s32[6]{0:T(128)S(1)} %concatenate.181.place, bf16[1024,1024]{1,0:T(8,128)(2,1)S(1)} %bitcast.129, bf16[1024,1152]{1,0:T(8,128)(2,1)S(1)} %bitcast.110, bf16[2,2048,768]{2,1,0:T(8,128)(2,1)S(1)} %bitcast.98), custom_call_target="tpu_custom_call" | custom-call | flops 3221225472 | bytes 10485760 | tf_op jit(solution)/shard_map/hidden_product/pallas_call | solution.py:149
  120.8 5.7 %hidden_product.4 = (bf16[2048,768]{1,0:T(8,128)(2,1)S(1)}, bf16[2048,768]{1,0:T(8,128)(2,1)S(1)}) custom-call(s32[6]{0:T(128)S(1)} %pad_add_fusion.place, bf16[1024,1024]{1,0:T(8,128)(2,1)S(1)} %bitcast.123, bf16[1024,1152]{1,0:T(8,128)(2,1)S(1)} %bitcast.107, bf16[2,2048,768]{2,1,0:T(8,128)(2,1)S(1)} %bitcast.99, ...), custom_call_target="tpu_custom_call", output_to_operand_aliasing={{0}: (4, {}), {1}: (5, {})} | custom-call | flops 3221225472 | bytes 10485760 | tf_op jit(solution)/shard_map/hidden_product/pallas_call | solution.py:149
  136.8 9.2 %back_product.2.own = bf16[2048,768]{1,0:T(8,128)(2,1)S(1)} custom-call(s32[6]{0:T(128)S(1)} %concatenate.181.place, bf16[2048,512]{1,0:T(8,128)(2,1)S(1)} %bitcast.118, bf16[2048,512]{1,0:T(8,128)(2,1)S(1)} %bitcast.115, bf16[2048,512]{1,0:T(8,128)(2,1)S(1)} %bitcast.126, bf16[2048,512]{1,0:T(8,128)(2,1)S(1)} %bitcast.120, ...), custom_call_target="tpu_custom_call" | custom-call | flops 6442450944 | bytes 17825792 | tf_op jit(solution)/shard_map/back_product/pallas_call | solution.py:201
  164.5 5.7 %hidden_product.5 = (bf16[1024,768]{1,0:T(8,128)(2,1)S(1)}, bf16[1024,768]{1,0:T(8,128)(2,1)S(1)}) custom-call(s32[6]{0:T(128)S(1)} %concatenate.188.place, bf16[1024,1024]{1,0:T(8,128)(2,1)S(1)} %bitcast.132, bf16[1024,1152]{1,0:T(8,128)(2,1)S(1)} %bitcast.113, bf16[2,2048,768]{2,1,0:T(8,128)(2,1)S(1)} %bitcast.100, ...), custom_call_target="tpu_custom_call" | custom-call | flops 3221225472 | bytes 10485760 | tf_op jit(solution)/shard_map/hidden_product/pallas_call | solution.py:149
  170.2 5.3 %back_product.3.rest = bf16[1024,768]{1,0:T(8,128)(2,1)S(1)} custom-call(s32[6]{0:T(128)S(1)} %concatenate.188.place, bf16[2048,512]{1,0:T(8,128)(2,1)S(1)} %bitcast.119, bf16[2048,512]{1,0:T(8,128)(2,1)S(1)} %bitcast.116, bf16[2048,512]{1,0:T(8,128)(2,1)S(1)} %bitcast.128, bf16[2048,512]{1,0:T(8,128)(2,1)S(1)} %bitcast.121, ...), custom_call_target="tpu_custom_call" | custom-call | flops 3221225472 | bytes 10485760 | tf_op jit(solution)/shard_map/back_product/pallas_call | solution.py:201
  175.4 9.4 %out_product.2 = bf16[1024,2048]{1,0:T(8,128)(2,1)S(1)} custom-call(s32[1]{0:T(128)} %bitcast.place, bf16[2048,768]{1,0:T(8,128)(2,1)S(1)} %get-tuple-element.12.own, bf16[1024,768]{1,0:T(8,128)(2,1)S(1)} %get-tuple-element.14.rest, bf16[2,2048,768]{2,1,0:T(8,128)(2,1)S(1)} %bitcast.106), custom_call_target="tpu_custom_call" | custom-call | flops 6442450944 | bytes 13631488 | tf_op jit(solution)/shard_map/out_product/pallas_call | solution.py:260
  187.5 9.4 %out_product.3 = bf16[1024,2048]{1,0:T(8,128)(2,1)S(1)} custom-call(s32[1]{0:T(128)} %bitcast.place, bf16[2048,768]{1,0:T(8,128)(2,1)S(1)} %copy-done.1, bf16[1024,768]{1,0:T(8,128)(2,1)S(1)} %back_product.3.rest, bf16[2,2048,768]{2,1,0:T(8,128)(2,1)S(1)} %bitcast.101), custom_call_target="tpu_custom_call" | custom-call | flops 6442450944 | bytes 13631488 | tf_op jit(solution)/shard_map/out_product/pallas_call | solution.py:260
  208.3 4.2 %all-to-all-start.2 = ((bf16[8,64,768]{2,1,0:T(8,128)(2,1)}), bf16[8,64,768]{2,1,0:T(8,128)(2,1)}, u32[]{:S(2)}, u32[]{:S(2)}) async-start(bf16[8,64,768]{2,1,0:T(8,128)(2,1)} %maximum_select_fusion.2), calls=%async_computation.2 | async-start | bytes 1572864 | tf_op jit(solution)/shard_map/all_to_all | solution.py:397
  215.3 7.7 %collective-permute-done.37 = bf16[512,384]{1,0:T(8,128)(2,1)} collective-permute-done((bf16[512,384]{1,0:T(8,128)(2,1)}, bf16[512,384]{1,0:T(8,128)(2,1)}, u32[]{:S(2)}, u32[]{:S(2)}) %collective-permute-start.37) | collective-permute-done | bytes 393248 | tf_op jit(solution)/shard_map/ppermute | solution.py:17
  232.5 3.8 %fusion.1.refs_1_ = bf16[4,128,2048]{2,1,0:T(8,128)(2,1)} fusion(bf16[4,128,2048]{2,1,0:T(8,128)(2,1)S(1)} %bitcast.134, bf16[4,128,2048]{2,1,0:T(8,128)(2,1)} %collective-permute-done.29), kind=kLoop, calls=%fused_computation.7 | loop fusion | flops 4194304 | bytes 6291456 | tf_op jit(solution)/shard_map/convert_element_type | solution.py:75
  247.0 19.2 %collective-permute-done.38 = bf16[512,384]{1,0:T(8,128)(2,1)} collective-permute-done((bf16[512,384]{1,0:T(8,128)(2,1)}, bf16[512,384]{1,0:T(8,128)(2,1)}, u32[]{:S(2)}, u32[]{:S(2)}) %collective-permute-start.38) | collective-permute-done | bytes 393248 | tf_op jit(solution)/shard_map/ppermute | solution.py:17
  269.3 4.5 %all-to-all-start = ((bf16[8,64,768]{2,1,0:T(8,128)(2,1)}), bf16[8,64,768]{2,1,0:T(8,128)(2,1)S(1)}, u32[]{:S(2)}, u32[]{:S(2)}) async-start(bf16[8,64,768]{2,1,0:T(8,128)(2,1)} %maximum_select_fusion), calls=%async_computation | async-start | bytes 1572864 | tf_op jit(solution)/shard_map/all_to_all | solution.py:397
  288.3 4.2 %all-to-all-start.1 = ((bf16[8,64,768]{2,1,0:T(8,128)(2,1)}), bf16[8,64,768]{2,1,0:T(8,128)(2,1)}, u32[]{:S(2)}, u32[]{:S(2)}) async-start(bf16[8,64,768]{2,1,0:T(8,128)(2,1)} %gather_fusion), calls=%async_computation.1 | async-start | bytes 1572864 | tf_op jit(solution)/shard_map/all_to_all | solution.py:398
  297.2 12.3 %collective-permute-done.32 = bf16[128,2048]{1,0:T(8,128)(2,1)} collective-permute-done((bf16[128,2048]{1,0:T(8,128)(2,1)}, bf16[128,2048]{1,0:T(8,128)(2,1)}, u32[]{:S(2)}, u32[]{:S(2)}) %collective-permute-start.32) | collective-permute-done | bytes 524320 | tf_op jit(solution)/shard_map/ppermute | solution.py:17
  311.8 5.7 %all-to-all-done.1 = bf16[8,64,768]{2,1,0:T(8,128)(2,1)} async-done(((bf16[8,64,768]{2,1,0:T(8,128)(2,1)}), bf16[8,64,768]{2,1,0:T(8,128)(2,1)}, u32[]{:S(2)}, u32[]{:S(2)}) %all-to-all-start.1) | async-done | bytes 786464 | tf_op jit(solution)/shard_map/all_to_all | solution.py:398
  (250 shorter events, 155.1 us)
Async XLA Ops:
  2.8 34.9 %collective-permute-start.5 = (bf16[1,128,1152]{2,1,0:T(8,128)(2,1)S(1)}, bf16[1,128,1152]{2,1,0:T(8,128)(2,1)S(1)}, u32[]{:S(2)}, u32[]{:S(2)}) collective-permute-start(bf16[1,128,1152]{2,1,0:T(8,128)(2,1)S(1)} %get-tuple-element.59), channel_id=1, source_target_pairs={{0,16},{8,24},{16,0},{24,8},{1,17},{9,25},{17,1},{25,9},{2,18},{10... | collective-permute-start | bytes 884744 | tf_op jit(solution)/shard_map/ppermute | solution.py:17
  6.9 32.1 %collective-permute-start.11 = (bf16[1,1,1,1,128,1152]{5,4,3,2,1,0:T(8,128)(2,1)S(1)}, bf16[1,1,1,1,128,1152]{5,4,3,2,1,0:T(8,128)(2,1)S(1)}, u32[]{:S(2)}, u32[]{:S(2)}) collective-permute-start(bf16[1,1,1,1,128,1152]{5,4,3,2,1,0:T(8,128)(2,1)S(1)} %get-tuple-element.58), channel_id=1, source_target_pairs={{0,2},{1,3},{2,0},{3,1},{4,6},{5,7},{6,4},{7,5},{8,10},{9,11},{10,... | collective-permute-start | bytes 884744 | tf_op jit(solution)/shard_map/ppermute | solution.py:17
  36.3 31.4 %collective-permute-start.9 = (bf16[1,1,2,1,128,1024]{5,4,3,2,1,0:T(8,128)(2,1)}, bf16[1,1,2,1,128,1024]{5,4,3,2,1,0:T(8,128)(2,1)}, u32[]{:S(2)}, u32[]{:S(2)}) collective-permute-start(bf16[1,1,2,1,128,1024]{5,4,3,2,1,0:T(8,128)(2,1)} %pad_maximum_fusion.21), channel_id=1, source_target_pairs={{0,2},{1,3},{2,0},{3,1},{4,6},{5,7},{6,4},{7,5},{8,10},{9,11},{10,... | collective-permute-start | bytes 1572872 | tf_op jit(solution)/shard_map/ppermute | solution.py:17
  39.9 30.0 %collective-permute-start.12 = (bf16[1,1,1,2,128,1152]{5,4,3,2,1,0:T(8,128)(2,1)}, bf16[1,1,1,2,128,1152]{5,4,3,2,1,0:T(8,128)(2,1)S(1)}, u32[]{:S(2)}, u32[]{:S(2)}) collective-permute-start(bf16[1,1,1,2,128,1152]{5,4,3,2,1,0:T(8,128)(2,1)} %pad_maximum_fusion.19), channel_id=1, source_target_pairs={{0,4},{1,5},{2,6},{3,7},{4,0},{5,1},{6,2},{7,3},{8,12},{9,13},{10,... | collective-permute-start | bytes 1769480 | tf_op jit(solution)/shard_map/ppermute | solution.py:17
  69.9 25.0 %collective-permute-start.24 = (bf16[2,1,1,2,128,512]{5,4,0,3,2,1:T(8,128)(2,1)S(1)}, bf16[2,1,1,2,128,512]{5,4,0,3,2,1:T(8,128)(2,1)S(1)}, u32[]{:S(2)}, u32[]{:S(2)}) collective-permute-start(bf16[2,1,1,2,128,512]{5,4,0,3,2,1:T(8,128)(2,1)S(1)} %pad_maximum_fusion.24), channel_id=1, source_target_pairs={{0,4},{1,5},{2,6},{3,7},{4,0},{5,1},{6,2},{7,3},{8,12},{9,13},{10,... | collective-permute-start | bytes 1572872 | tf_op jit(solution)/shard_map/ppermute | solution.py:17
  75.7 32.1 %collective-permute-start.10 = (bf16[1,1,2,2,128,1024]{5,4,3,2,1,0:T(8,128)(2,1)S(1)}, bf16[1,1,2,2,128,1024]{5,4,3,2,1,0:T(8,128)(2,1)S(1)}, u32[]{:S(2)}, u32[]{:S(2)}) collective-permute-start(bf16[1,1,2,2,128,1024]{5,4,3,2,1,0:T(8,128)(2,1)S(1)} %pad_maximum_fusion.13), channel_id=1, source_target_pairs={{0,1},{1,0},{2,3},{3,2},{4,5},{5,4},{6,7},{7,6},{8,9},{9,8},{10,11... | collective-permute-start | bytes 3145736 | tf_op jit(solution)/shard_map/ppermute | solution.py:17
  80.0 29.7 %collective-permute-start.13 = (bf16[1,1,2,2,128,1152]{5,4,3,2,1,0:T(8,128)(2,1)S(1)}, bf16[1,1,2,2,128,1152]{5,4,3,2,1,0:T(8,128)(2,1)S(1)}, u32[]{:S(2)}, u32[]{:S(2)}) collective-permute-start(bf16[1,1,2,2,128,1152]{5,4,3,2,1,0:T(8,128)(2,1)S(1)} %pad_maximum_fusion.11), channel_id=1, source_target_pairs={{0,1},{1,0},{2,3},{3,2},{4,5},{5,4},{6,7},{7,6},{8,9},{9,8},{10,11... | collective-permute-start | bytes 3538952 | tf_op jit(solution)/shard_map/ppermute | solution.py:17
  109.8 23.5 %collective-permute-start.19 = (bf16[2,1,2,2,128,512]{5,4,0,3,2,1:T(8,128)(2,1)S(1)}, bf16[2,1,2,2,128,512]{5,4,0,3,2,1:T(8,128)(2,1)S(1)}, u32[]{:S(2)}, u32[]{:S(2)}) collective-permute-start(bf16[2,1,2,2,128,512]{5,4,0,3,2,1:T(8,128)(2,1)S(1)} %pad_maximum_fusion.14), channel_id=1, source_target_pairs={{0,1},{1,0},{2,3},{3,2},{4,5},{5,4},{6,7},{7,6},{8,9},{9,8},{10,11... | collective-permute-start | bytes 3145736 | tf_op jit(solution)/shard_map/ppermute | solution.py:17
  128.4 33.4 %collective-permute-start.22 = (bf16[512,768]{1,0:T(8,128)(2,1)S(1)}, bf16[512,768]{1,0:T(8,128)(2,1)}, u32[]{:S(2)}, u32[]{:S(2)}) collective-permute-start(bf16[512,768]{1,0:T(8,128)(2,1)S(1)} %multiply_convert_fusion.3.refs_6_), channel_id=1, source_target_pairs={{0,8},{8,0},{16,24},{24,16},{1,9},{9,1},{17,25},{25,17},{2,10},{10... | collective-permute-start | bytes 2359304 | tf_op jit(solution)/shard_map/ppermute | solution.py:17
  133.1 66.3 %collective-permute-start.44 = (bf16[512,768]{1,0:T(8,128)(2,1)}, bf16[512,768]{1,0:T(8,128)(2,1)}, u32[]{:S(2)}, u32[]{:S(2)}) collective-permute-start(bf16[512,768]{1,0:T(8,128)(2,1)} %multiply_convert_fusion.2.refs_7_), channel_id=1, source_target_pairs={{0,8},{8,0},{16,24},{24,16},{1,9},{9,1},{17,25},{25,17},{2,10},{10... | collective-permute-start | bytes 2359304 | tf_op jit(solution)/shard_map/ppermute | solution.py:17
  152.5 54.6 %collective-permute-start.39 = (bf16[512,384]{1,0:T(8,128)(2,1)S(1)}, bf16[512,384]{1,0:T(8,128)(2,1)}, u32[]{:S(2)}, u32[]{:S(2)}) collective-permute-start(bf16[512,384]{1,0:T(8,128)(2,1)S(1)} %get-tuple-element.48), channel_id=1, source_target_pairs={{0,8},{8,0},{16,24},{24,16},{1,9},{9,1},{17,25},{25,17},{2,10},{10... | collective-permute-start | bytes 1179656 | tf_op jit(solution)/shard_map/ppermute | solution.py:17
  154.5 58.0 %collective-permute-start.42 = (bf16[512,384]{1,0:T(8,128)(2,1)S(1)}, bf16[512,384]{1,0:T(8,128)(2,1)}, u32[]{:S(2)}, u32[]{:S(2)}) collective-permute-start(bf16[512,384]{1,0:T(8,128)(2,1)S(1)} %get-tuple-element.49.rest_2_), channel_id=1, source_target_pairs={{0,8},{8,0},{16,24},{24,16},{1,9},{9,1},{17,25},{25,17},{2,10},{10... | collective-permute-start | bytes 1179656 | tf_op jit(solution)/shard_map/ppermute | solution.py:17
  163.1 40.0 %collective-permute-start.43 = (bf16[512,768]{1,0:T(8,128)(2,1)S(1)}, bf16[512,768]{1,0:T(8,128)(2,1)}, u32[]{:S(2)}, u32[]{:S(2)}) collective-permute-start(bf16[512,768]{1,0:T(8,128)(2,1)S(1)} %add_convert_fusion.1.rest_0_), channel_id=1, source_target_pairs={{0,16},{8,24},{16,0},{24,8},{1,17},{9,25},{17,1},{25,9},{2,18},{10... | collective-permute-start | bytes 2359304 | tf_op jit(solution)/shard_map/ppermute | solution.py:17
  196.8 35.6 %collective-permute-start.29 = (bf16[4,128,2048]{2,1,0:T(8,128)(2,1)}, bf16[4,128,2048]{2,1,0:T(8,128)(2,1)}, u32[]{:S(2)}, u32[]{:S(2)}) collective-permute-start(bf16[4,128,2048]{2,1,0:T(8,128)(2,1)} %bitcast.36), channel_id=1, source_target_pairs={{0,1},{1,0},{2,3},{3,2},{4,5},{5,4},{6,7},{7,6},{8,9},{9,8},{10,11... | collective-permute-start | bytes 6291464 | tf_op jit(solution)/shard_map/ppermute | solution.py:17
  199.5 38.3 %collective-permute-start.33 = (bf16[4,128,2048]{2,1,0:T(8,128)(2,1)}, bf16[4,128,2048]{2,1,0:T(8,128)(2,1)}, u32[]{:S(2)}, u32[]{:S(2)}) collective-permute-start(bf16[4,128,2048]{2,1,0:T(8,128)(2,1)} %bitcast.42), channel_id=1, source_target_pairs={{0,1},{1,0},{2,3},{3,2},{4,5},{5,4},{6,7},{7,6},{8,9},{9,8},{10,11... | collective-permute-start | bytes 6291464 | tf_op jit(solution)/shard_map/ppermute | solution.py:17
  228.9 39.5 %all-to-all-start.3 = ((bf16[8,64,768]{2,1,0:T(8,128)(2,1)}), bf16[8,64,768]{2,1,0:T(8,128)(2,1)S(1)}, u32[]{:S(2)}, u32[]{:S(2)}) async-start(bf16[8,64,768]{2,1,0:T(8,128)(2,1)} %gather_fusion.1), calls=%async_computation.3 | async-start | bytes 1572864 | tf_op jit(solution)/shard_map/all_to_all | solution.py:398
  236.2 30.0 %collective-permute-start.38 = (bf16[512,384]{1,0:T(8,128)(2,1)}, bf16[512,384]{1,0:T(8,128)(2,1)}, u32[]{:S(2)}, u32[]{:S(2)}) collective-permute-start(bf16[512,384]{1,0:T(8,128)(2,1)} %after.19), channel_id=1, source_target_pairs={{0,16},{8,24},{16,0},{24,8},{1,17},{9,25},{17,1},{25,9},{2,18},{10... | collective-permute-start | bytes 1179656 | tf_op jit(solution)/shard_map/ppermute | solution.py:17
  242.0 39.5 %collective-permute-start.34 = (bf16[128,2048]{1,0:T(8,128)(2,1)}, bf16[128,2048]{1,0:T(8,128)(2,1)}, u32[]{:S(2)}, u32[]{:S(2)}) collective-permute-start(bf16[128,2048]{1,0:T(8,128)(2,1)} %get-tuple-element.32), channel_id=1, source_target_pairs={{0,2},{1,3},{2,0},{3,1},{4,6},{5,7},{6,4},{7,5},{8,10},{9,11},{10,... | collective-permute-start | bytes 1572872 | tf_op jit(solution)/shard_map/ppermute | solution.py:17
  243.9 48.6 %collective-permute-start.36 = (bf16[128,2048]{1,0:T(8,128)(2,1)}, bf16[128,2048]{1,0:T(8,128)(2,1)}, u32[]{:S(2)}, u32[]{:S(2)}) collective-permute-start(bf16[128,2048]{1,0:T(8,128)(2,1)} %get-tuple-element.33), channel_id=1, source_target_pairs={{0,6},{1,7},{2,4},{3,5},{4,2},{5,3},{6,0},{7,1},{8,14},{9,15},{10,... | collective-permute-start | bytes 1572872 | tf_op jit(solution)/shard_map/ppermute | solution.py:17
  245.4 47.1 %collective-permute-start.35 = (bf16[128,2048]{1,0:T(8,128)(2,1)}, bf16[128,2048]{1,0:T(8,128)(2,1)}, u32[]{:S(2)}, u32[]{:S(2)}) collective-permute-start(bf16[128,2048]{1,0:T(8,128)(2,1)} %get-tuple-element.34), channel_id=1, source_target_pairs={{0,4},{1,5},{2,6},{3,7},{4,0},{5,1},{6,2},{7,3},{8,12},{9,13},{10,... | collective-permute-start | bytes 1572872 | tf_op jit(solution)/shard_map/ppermute | solution.py:17
  245.5 34.4 %collective-permute-start.41 = (bf16[512,384]{1,0:T(8,128)(2,1)}, bf16[512,384]{1,0:T(8,128)(2,1)}, u32[]{:S(2)}, u32[]{:S(2)}) collective-permute-start(bf16[512,384]{1,0:T(8,128)(2,1)} %after.21), channel_id=1, source_target_pairs={{0,16},{8,24},{16,0},{24,8},{1,17},{9,25},{17,1},{25,9},{2,18},{10... | collective-permute-start | bytes 1179656 | tf_op jit(solution)/shard_map/ppermute | solution.py:17
  280.0 29.5 %collective-permute-start.32 = (bf16[128,2048]{1,0:T(8,128)(2,1)}, bf16[128,2048]{1,0:T(8,128)(2,1)}, u32[]{:S(2)}, u32[]{:S(2)}) collective-permute-start(bf16[128,2048]{1,0:T(8,128)(2,1)} %get-tuple-element.36), channel_id=1, source_target_pairs={{0,6},{1,7},{2,4},{3,5},{4,2},{5,3},{6,0},{7,1},{8,14},{9,15},{10,... | collective-permute-start | bytes 1572872 | tf_op jit(solution)/shard_map/ppermute | solution.py:17
  281.6 27.9 %collective-permute-start.31 = (bf16[128,2048]{1,0:T(8,128)(2,1)}, bf16[128,2048]{1,0:T(8,128)(2,1)}, u32[]{:S(2)}, u32[]{:S(2)}) collective-permute-start(bf16[128,2048]{1,0:T(8,128)(2,1)} %get-tuple-element.37), channel_id=1, source_target_pairs={{0,4},{1,5},{2,6},{3,7},{4,0},{5,1},{6,2},{7,3},{8,12},{9,13},{10,... | collective-permute-start | bytes 1572872 | tf_op jit(solution)/shard_map/ppermute | solution.py:17
  288.3 29.1 %all-to-all-start.1 = ((bf16[8,64,768]{2,1,0:T(8,128)(2,1)}), bf16[8,64,768]{2,1,0:T(8,128)(2,1)}, u32[]{:S(2)}, u32[]{:S(2)}) async-start(bf16[8,64,768]{2,1,0:T(8,128)(2,1)} %gather_fusion), calls=%async_computation.1 | async-start | bytes 1572864 | tf_op jit(solution)/shard_map/all_to_all | solution.py:398
  (60 other events, 659.9 us)
